TPU v7x, 128 devices: a whole 4x4x4 slice. The times are simulated.
128 devices in a mesh: dp: 8 (over z, x_hi), fsdp: 16 (over y, x_lo, core).
Axes of the slice: x: 4 (x_hi: 2, x_lo: 2; x = x_hi * 2 + x_lo), y: 4, z: 4, core: 2. Of those that a mesh axis runs over, the one named last changes fastest.
Arguments:
- old_weight: float32 [8192, 14336], P(('dp', 'fsdp')), may hold values from -6 to 6
- old_first: float32 [8192, 14336], P(('dp', 'fsdp')), may hold values from -2 to 2
- old_second: float32 [8192, 14336], P(('dp', 'fsdp')), may hold values from 0.05 to 2
- tokens: bfloat16 [4096, 8192], P(('dp', 'fsdp')), may hold values from -24 to 24
- cotangent: bfloat16 [4096, 14336], P('dp', 'fsdp'), may hold values from -24 to 24
Outputs:
- new_weight: float32 [8192, 14336], P('dp', 'fsdp')
- new_first: float32 [8192, 14336], P('dp', 'fsdp')
- new_second: float32 [8192, 14336], P('dp', 'fsdp')
- norm_rows: float32 [4096], P(('dp', 'fsdp'))
All inputs are finite; a program needn't handle non-finite values.
Results may differ from a plain program's by a relative error of at most 0.019.
Values may be sent and summed in bfloat16 or wider, within the bound.
A program may use at most 128 MiB of HBM per device.

v0:
```python
import jax
import jax.numpy as jnp
from jax import lax
from jax.sharding import PartitionSpec as P

D = 8192
FF = 14336


def body(old_weight, old_first, old_second, tokens, cotangent):
    fan_scale = D ** (-0.5)
    weight_tile, first_tile, second_tile = (
        lax.all_to_all(
            old_weight.astype(jnp.bfloat16), "fsdp", split_axis=1, concat_axis=0, tiled=True
        ).astype(old_weight.dtype),
        lax.all_to_all(
            old_first.astype(jnp.bfloat16), "fsdp", split_axis=1, concat_axis=0, tiled=True
        ).astype(old_first.dtype),
        lax.all_to_all(
            old_second.astype(jnp.bfloat16), "fsdp", split_axis=1, concat_axis=0, tiled=True
        ).astype(old_second.dtype),
    )
    group_rows = lax.all_gather(tokens, "fsdp", axis=0, tiled=True)
    weight_low = weight_tile.astype(jnp.bfloat16)
    token_cols = group_rows
    preact = (
        jnp.dot(
            token_cols,
            lax.all_gather(weight_low, "dp", axis=0, tiled=True),
            preferred_element_type=jnp.float32,
        )
        * fan_scale
    )
    gate_sig = jax.nn.sigmoid(preact)
    hidden = preact * gate_sig
    square_total = lax.psum_scatter(
        jnp.sum(hidden * hidden, axis=1), "fsdp", scatter_dimension=0, tiled=True
    )
    norm_rows = jnp.sqrt(square_total / FF + 1e-06)
    slope = (cotangent.astype(jnp.float32) * gate_sig * (1.0 + preact * (1.0 - gate_sig))).astype(
        jnp.bfloat16
    )
    token_cols = group_rows
    grad = lax.psum_scatter(
        (
            lax.dot_general(
                token_cols, slope, (((0,), (0,)), ((), ())), preferred_element_type=jnp.float32
            )
            * fan_scale
        ).astype(jnp.bfloat16),
        "dp",
        scatter_dimension=0,
        tiled=True,
    ).astype(jnp.float32)
    new_first = 0.9 * first_tile + 0.1 * grad
    new_second = 0.95 * second_tile + 0.05 * grad * grad
    update = new_first / (1.0 - 0.9**10) / (jnp.sqrt(new_second / (1.0 - 0.95**10)) + 1e-08)
    new_weight = weight_tile - 0.02 * (update + 0.1 * weight_tile)
    return (new_weight, new_first, new_second, norm_rows)


def solution(mesh):
    placed = (
        P(("dp", "fsdp"), None),
        P(("dp", "fsdp"), None),
        P(("dp", "fsdp"), None),
        P(("dp", "fsdp"), None),
        P("dp", "fsdp"),
    )
    return jax.shard_map(
        body,
        mesh=mesh,
        in_specs=placed,
        out_specs=(P("dp", "fsdp"), P("dp", "fsdp"), P("dp", "fsdp"), P(("dp", "fsdp"))),
        check_vma=False,
    )
```

profile of v0, /device:TPU:0, one launch (start us, length us, event | category | flops | bytes accessed | tf_op | source)
XLA Modules:
  0.0 515.2 jit_solution(15712300327269508293)
XLA Ops:
  7.9 2.2 convert_element_type.38
  10.4 44.9 %all_to_all.45 = bf16[64,16,896]{2,0,1:T(8,128)(2,1)} all-to-all(bf16[64,16,896]{2,0,1:T(8,128)(2,1)S(1)} %bitcast.32), channel_id=1, replica_groups=mesh['dp'=8,'fsdp'=16] {'fsdp'}, dimensions={1} | all-to-all | bytes 3670016 | tf_op jit(solution)/shard_map/all_to_all | solution.py:13
  55.4 24.2 %all-gather.3.cloned.1.call-done = bf16[512,8192]{1,0:T(8,128)(2,1)} async-done(((bf16[32,8192]{1,0:T(8,128)(2,1)}), bf16[512,8192]{1,0:T(8,128)(2,1)}) %all-gather.3.cloned.1.call-update) | async-done | bytes 8388624 | tf_op jit(solution)/shard_map/all_gather | solution.py:23
  79.7 167.9 %all-gather.5.cloned.1.call-done = bf16[8192,896]{1,0:T(8,128)(2,1)} async-done(((bf16[1024,896]{1,0:T(8,128)(2,1)}), bf16[8192,896]{1,0:T(8,128)(2,1)}) %all-gather.5.cloned.1.call-update) | async-done | bytes 14680080 | tf_op jit(solution)/shard_map/all_gather | solution.py:29
  247.6 19.7 %multiply_reduce_fusion = (f32[512]{0:T(512)S(1)}, f32[512,896]{1,0:T(8,128)S(1)}) fusion(bf16[512,8192]{1,0:T(8,128)(2,1)} %all-gather.3.cloned.1.call-done, bf16[8192,896]{1,0:T(8,128)(2,1)} %all-gather.5.cloned.1.call-done), kind=kOutput, calls=%fused_computation.15 | convolution fusion | flops 7519403520 | bytes 24905728 | tf_op jit(solution)/shard_map/dot_general | solution.py:27
  267.3 12.1 %fusion = bf16[8192,896]{0,1:T(8,128)(2,1)} fusion(bf16[512,8192]{1,0:T(8,128)(2,1)S(1)} %copy-done.2, bf16[512,896]{1,0:T(8,128)(2,1)S(1)} %copy-done.3, f32[512,896]{1,0:T(8,128)S(1)} %get-tuple-element.24), kind=kOutput, calls=%fused_computation.1 | convolution fusion | flops 7535919104 | bytes 25821184 | tf_op jit(solution)/shard_map/dot_general | solution.py:46
  279.4 2.2 convert_element_type.40
  281.6 1.5 copy.46
  283.1 4.5 all-to-all-start.1
  287.6 2.3 convert_element_type.47
  291.5 38.6 %all-to-all-done.1 = bf16[64,16,896]{2,0,1:T(8,128)(2,1)} async-done(((bf16[64,16,896]{2,0,1:T(8,128)(2,1)}), bf16[64,16,896]{2,0,1:T(8,128)(2,1)}, u32[]{:S(2)}, u32[]{:S(2)}) %all-to-all-start.1) | async-done | bytes 1835040 | tf_op jit(solution)/shard_map/all_to_all | solution.py:16
  330.0 4.4 all-to-all-start.2
  335.7 2.5 copy.31
  338.3 3.7 convert_multiply_fusion.3
  342.0 5.3 %copy.33 = f32[1024,896]{0,1:T(8,128)} copy(f32[1024,896]{1,0:T(8,128)} %bitcast.29) | data formatting | bytes 7340032 | tf_op jit(solution)/shard_map/mul | solution.py:55
  347.3 29.0 %all-to-all-done.2 = bf16[64,16,896]{2,0,1:T(8,128)(2,1)} async-done(((bf16[64,16,896]{2,0,1:T(8,128)(2,1)}), bf16[64,16,896]{2,0,1:T(8,128)(2,1)}, u32[]{:S(2)}, u32[]{:S(2)}) %all-to-all-start.2) | async-done | bytes 1835040 | tf_op jit(solution)/shard_map/all_to_all | solution.py:19
  376.3 3.7 convert_multiply_fusion.2
  380.0 5.3 %copy.35 = f32[1024,896]{0,1:T(8,128)} copy(f32[1024,896]{1,0:T(8,128)} %bitcast.30) | data formatting | bytes 7340032 | tf_op jit(solution)/shard_map/mul | solution.py:56
  385.3 27.7 %all-reduce = f32[512]{0:T(512)S(1)} all-reduce(f32[512]{0:T(512)S(1)} %get-tuple-element.23), channel_id=3, replica_groups=mesh['dp'=8,'fsdp'=16] {'fsdp'}, use_global_device_ids=true, to_apply=%region_2.0.clone | all-reduce | flops 512 | bytes 4096
  413.5 72.6 %reduce-scatter.2.cloned.1.call-done = bf16[1024,896]{0,1:T(8,128)(2,1)} async-done(((bf16[8192,896]{0,1:T(8,128)(2,1)}), bf16[1024,896]{0,1:T(8,128)(2,1)}) %reduce-scatter.2.cloned.1.call-update) | async-done | bytes 1835024 | tf_op jit(solution)/shard_map/reduce_scatter | solution.py:44
  486.1 7.6 %convert_subtract_fusion = (f32[1024,896]{0,1:T(8,128)}, f32[1024,896]{0,1:T(8,128)}, f32[1024,896]{0,1:T(8,128)}) fusion(bf16[1024,896]{0,1:T(8,128)(2,1)S(1)} %copy-done.1, f32[1024,896]{0,1:T(8,128)} %copy.33, bf16[1024,896]{0,1:T(8,128)(2,1)} %reduce-scatter.2.cloned.1.call-done, f32[1024,896]{0,1:T(8,128)} %copy.35), kind=kLoop, calls=%fused_computation.4 | loop fusion | flops 13762560 | bytes 22020096 | tf_op jit(solution)/shard_map/sub | solution.py:58
  493.7 5.0 copy.36
  498.7 5.0 copy.37
  503.7 5.0 copy.38
  (20 shorter events, 3.8 us)
Async XLA Ops:
  7.2 72.5 %all-gather.3.cloned.1.call-start = ((), (), s32[]{:S(2)}) async-start(), calls=%async_computation.4 | async-start | bytes 8912896 | tf_op jit(solution)/shard_map/all_gather | solution.py:23
  7.9 239.7 %all-gather.5.cloned.1.call-start = ((), (), s32[]{:S(2)}) async-start(), calls=%async_computation.5 | async-start | bytes 16515072 | tf_op jit(solution)/shard_map/all_gather | solution.py:29
  55.4 211.9 %copy-start.3 = (bf16[512,896]{1,0:T(8,128)(2,1)S(1)}, bf16[512,896]{1,0:T(8,128)(2,1)}, u32[]{:S(2)}) copy-start(bf16[512,896]{1,0:T(8,128)(2,1)} %param.9) | copy-start | bytes 2752516
  55.4 430.8 %reduce-scatter.2.cloned.1.call-start = ((), (), s32[]{:S(2)}) async-start(), calls=%async_computation.6 | async-start | bytes 16515072 | tf_op jit(solution)/shard_map/reduce_scatter | solution.py:44
  247.6 19.7 %copy-start.2 = (bf16[512,8192]{1,0:T(8,128)(2,1)S(1)}, bf16[512,8192]{1,0:T(8,128)(2,1)}, u32[]{:S(2)}) copy-start(bf16[512,8192]{1,0:T(8,128)(2,1)} %all-gather.3.cloned.1.call-done) | copy-start | bytes 25165828
  283.1 46.9 %all-to-all-start.1 = ((bf16[64,16,896]{2,0,1:T(8,128)(2,1)}), bf16[64,16,896]{2,0,1:T(8,128)(2,1)}, u32[]{:S(2)}, u32[]{:S(2)}) async-start(bf16[64,16,896]{2,0,1:T(8,128)(2,1)} %bitcast.25), calls=%async_computation.1 | async-start | bytes 3670016 | tf_op jit(solution)/shard_map/all_to_all | solution.py:16
  289.9 44.5 %copy-start.4 = (u32[128]{0:T(128)S(1)}, u32[128]{0:T(128)}, u32[]{:S(2)}) copy-start(u32[128]{0:T(128)} %constant.36) | copy-start | bytes 1540
  289.9 45.8 %copy-start = (bf16[64,16,896]{2,0,1:T(8,128)(2,1)S(1)}, bf16[64,16,896]{2,0,1:T(8,128)(2,1)}, u32[]{:S(2)}) copy-start(bf16[64,16,896]{2,0,1:T(8,128)(2,1)} %all_to_all.45) | copy-start | bytes 5505028
  330.0 46.2 %all-to-all-start.2 = ((bf16[64,16,896]{2,0,1:T(8,128)(2,1)}), bf16[64,16,896]{2,0,1:T(8,128)(2,1)}, u32[]{:S(2)}, u32[]{:S(2)}) async-start(bf16[64,16,896]{2,0,1:T(8,128)(2,1)} %bitcast.31), calls=%async_computation.3 | async-start | bytes 3670016 | tf_op jit(solution)/shard_map/all_to_all | solution.py:19
  380.0 106.1 %copy-start.1 = (bf16[1024,896]{0,1:T(8,128)(2,1)S(1)}, bf16[1024,896]{0,1:T(8,128)(2,1)}, u32[]{:S(2)}) copy-start(bf16[1024,896]{0,1:T(8,128)(2,1)} %copy.31) | copy-start | bytes 5505028
Sparse Core Ops, SparseCore 0:
  9.7 69.9 all-gather.2
  82.0 165.5 all-gather.4
  279.5 206.5 reduce-scatter.1
where the time goes:
time: 516 us; the launch traced here: 515 us
  waiting for transfers between devices  333 us (65%)
  blocking collectives  72.5 us (14%)
  local copies, waits for them, and re-layouts  32 us (6%)
  matrix products  31.7 us (6%)
  other arithmetic  22.4 us (4%)
  between operations  14.5 us (3%)
  starting transfers between devices  9.01 us (2%)
    all_gather x1, waiting for transfers between devices, body(): lax.all_gather(weight_low, 'dp', axis=0, tiled=True)  168 us
    reduce_scatter x1, waiting for transfers between devices, body(): lax.psum_scatter((lax.dot_general(token_cols, slope, (((0,), (0,)), ((),...  72.6 us
    all_to_all x1, blocking collectives, body(): lax.all_to_all(old_weight.astype(jnp.bfloat16), 'fsdp', split_axis=1, con...  44.9 us
    all_to_all x1, waiting for transfers between devices, body(): lax.all_to_all(old_first.astype(jnp.bfloat16), 'fsdp', split_axis=1, conc...  38.6 us
    all_to_all x1, waiting for transfers between devices, body(): lax.all_to_all(old_second.astype(jnp.bfloat16), 'fsdp', split_axis=1, con...  29 us
    unnamed x1, blocking collectives  27.7 us
    all_gather x1, waiting for transfers between devices, body(): group_rows = lax.all_gather(tokens, 'fsdp', axis=0, tiled=True)  24.2 us
    dot_general x1, matrix products, body(): jnp.dot(token_cols, lax.all_gather(weight_low, 'dp', axis=0, tiled=True),...  19.7 us
  transfers between devices with their start and end apart: 5, of which 5 were waited for; matrix products, arithmetic and copies ran while one was open for 6% of the time, Pallas kernels for 0%

commit v1 on v0

v1 whole, which is shorter than its diff:
```python
import functools

import jax
import jax.numpy as jnp
from jax import lax
from jax.experimental import pallas as pl
from jax.experimental.pallas import tpu as pltpu
from jax.sharding import PartitionSpec as P

D = 8192
FF = 14336
SCALE = D ** (-0.5)
NF = 16
NZ = 4
GRP = 32
TC = 1024
FC = 896
SR = 64
TOKEN_LEAD = 2
LAG_X, LAG_S, LAG_Z, LAG_G = 2, 3, 4, 6
FIRST_AT, SECOND_AT = 2, 5
MESH = pl.DeviceIdType.MESH
BF, F32 = jnp.bfloat16, jnp.float32


def step_kernel(
    tok, cot, old_w, old_m, old_v,
    out_w, out_m, out_v, out_g, out_n,
    T, W, PS, RR, XO, XS, XR, SL, ACC, ST, CB, NS, NR,
    ld_sem, st_send, st_recv, own_sem, t1_send, t1_recv, tk_send, fw_send, tk_recv,
    rs_send, rs_recv, x_send, x_recv, s_send, s_recv, z_send, z_recv, n_send, n_recv,
):
    d, f = lax.axis_index("dp"), lax.axis_index("fsdp")
    z, xh = lax.div(d, 2), lax.rem(d, 2)
    y, xl, c = lax.div(f, 4), lax.rem(lax.div(f, 2), 2), lax.rem(f, 2)

    def at_f(dy, dxl, dc):
        return lax.rem(y + dy, 4) * 4 + lax.rem(xl + dxl, 2) * 2 + lax.rem(c + dc, 2)

    def piece(s):
        return at_f(lax.div(s, 4), lax.rem(lax.div(s, 2), 2), lax.rem(s, 2))

    def at_d(dz, dxh):
        return lax.rem(z + dz, NZ) * 2 + lax.rem(xh + dxh, 2)

    def remote(src, dst, send, recv, dev):
        return pltpu.make_async_remote_copy(
            src_ref=src, dst_ref=dst, send_sem=send, recv_sem=recv, device_id=dev, device_id_type=MESH
        )

    def rows(start, size):
        return pl.ds(pl.multiple_of(start, 32), size)

    def load(old, k):
        cols = pl.ds(pl.multiple_of(piece(k) * FC, 128), FC)
        return pltpu.make_async_copy(old.at[:, cols], ST.at[k], ld_sem.at[k])

    def load_all(old):
        def go(k, _):
            load(old, k).start()
            return 0

        lax.fori_loop(0, NF, go, 0)

    def state_copy(i, dst, k):
        return remote(
            CB.at[i, k], dst.at[rows(f * SR, SR)], st_send.at[i, k], st_recv.at[i, f], (d, piece(k))
        )

    def state_landed(i, dst, k):
        q = piece(k)
        return remote(CB.at[i, k], dst.at[rows(q * SR, SR)], st_send.at[i, k], st_recv.at[i, q], (d, q))

    def send_state(i, old, dst):
        def go(n, _):
            k = NF - 1 - n
            load(old, k).wait()
            CB[i, k] = ST[k].astype(BF)

            @pl.when(k > 0)
            def _():
                state_copy(i, dst, k).start()

            return 0

        lax.fori_loop(0, NF, go, 0)

    def own_state(i, dst):
        return pltpu.make_async_copy(CB.at[i, 0], dst.at[rows(f * SR, SR)], own_sem.at[i])

    load_all(old_w)

    barrier = pltpu.get_barrier_semaphore()

    def greet_f(k, _):
        pl.semaphore_signal(barrier, inc=1, device_id=(d, piece(k)), device_id_type=MESH)
        return 0

    lax.fori_loop(1, NF, greet_f, 0)

    def greet_d(k, _):
        pl.semaphore_signal(barrier, inc=1, device_id=(lax.rem(d + k, 8), f), device_id_type=MESH)
        return 0

    lax.fori_loop(1, 8, greet_d, 0)
    pl.semaphore_wait(barrier, NF - 1 + 7)

    def t1_copy(k):
        q = lax.rem(d + k, 8)
        cols = pl.ds(pl.multiple_of(q * TC, 128), TC)
        return remote(
            tok.at[:, cols], T.at[f, rows(d * GRP, GRP)], t1_send.at[k], t1_recv.at[d], (q, f)
        )

    def t1_landed(k):
        q = lax.rem(d + k, 8)
        return remote(
            tok.at[:, pl.ds(0, TC)], T.at[f, rows(q * GRP, GRP)], t1_send.at[k], t1_recv.at[q], (q, f)
        )

    def t1_go(k, _):
        t1_copy(k).start()
        return 0

    lax.fori_loop(1, 8, t1_go, 0)
    T[f, rows(d * GRP, GRP)] = tok[:, pl.ds(pl.multiple_of(d * TC, 128), TC)]

    send_state(0, old_w, W)
    own_state(0, W).start()
    load_all(old_m)

    def t1_wait(k, _):
        t1_landed(k).wait_recv()
        return 0

    lax.fori_loop(1, 8, t1_wait, 0)

    def token_copy(q, send, dev_f):
        return remote(T.at[q], T.at[q], send, tk_recv.at[q], (d, dev_f))

    def landed(q):
        return remote(T.at[q], T.at[q], tk_send.at[0], tk_recv.at[q], (d, at_f(0, 0, 1)))

    sibling = at_f(0, 0, 1)
    partner = at_f(0, 1, 0)
    first_sends = [token_copy(f, tk_send.at[0], partner)]
    first_sends += [token_copy(f, tk_send.at[j], at_f(dy, 0, 0)) for j, dy in ((1, 2), (2, 1), (3, 3))]
    first_sends += [token_copy(f, tk_send.at[4], sibling)]
    second_sends = [token_copy(partner, tk_send.at[4 + j], at_f(dy, 0, 0)) for j, dy in ((1, 2), (2, 1), (3, 3))]
    second_sends += [token_copy(partner, tk_send.at[8], sibling)]
    for copy in first_sends:
        copy.start()
    landed(partner).wait_recv()
    for copy in second_sends:
        copy.start()

    own_state(0, W).wait()

    def w_wait(k, _):
        state_landed(0, W, k).wait_recv()
        return 0

    lax.fori_loop(1, NF, w_wait, 0)
    w_out = pltpu.make_async_copy(W, out_w, own_sem.at[3])
    w_out.start()

    ACC[...] = jnp.zeros_like(ACC)

    def rs_copy(s, dz):
        zz = lax.rem(z + dz, NZ)
        return remote(
            PS.at[s, rows(zz * 64, 64)], RR.at[dz - 1, s], rs_send.at[dz - 1, s], rs_recv.at[dz - 1, s],
            (at_d(dz, 0), f),
        )

    def x_copy(s):
        return remote(XS.at[s], XR.at[s], x_send.at[s], x_recv.at[s], (at_d(0, 1), f))

    def s_copy(s):
        mine = SL.at[s, rows(d * GRP, GRP)]
        return remote(mine, mine, s_send.at[s], s_recv.at[s], (at_d(0, 1), f))

    def z_copy(s, dz):
        mine = SL.at[s, rows(z * 64, 64)]
        return remote(mine, mine, z_send.at[dz - 1, s], z_recv.at[dz - 1, s], (at_d(dz, 0), f))

    def n_copy(s):
        return remote(NS.at[s], NR.at[f], n_send.at[s], n_recv.at[f], (d, piece(s)))

    def n_landed(s):
        q = piece(s)
        return remote(NS.at[s], NR.at[q], n_send.at[s], n_recv.at[q], (d, q))

    def tokens_on(j):
        @pl.when((lax.rem(j, 2) == 0) & (j >= 4) & (j < NF))
        def _():
            q = piece(j)
            landed(q).wait_recv()
            token_copy(q, fw_send.at[j], sibling).start()

    def forward(s):
        q = piece(s)

        @pl.when(lax.rem(s, 2) == 1)
        def _():
            landed(q).wait_recv()

        part = jnp.dot(T[q], W[...], preferred_element_type=F32) * SCALE
        PS[s] = part.astype(BF)
        for dz in (2, 1, 3):
            rs_copy(s, dz).start()

    def reduce_z(s):
        for dz in (1, 3, 2):
            rs_copy(s, dz).wait_recv()

        def half(h):
            own = PS[s, rows(z * 64 + h * GRP, GRP)].astype(F32)
            here = rows(h * GRP, GRP)
            return own + RR[0, s, here].astype(F32) + RR[1, s, here].astype(F32) + RR[2, s, here].astype(F32)

        XS[s] = half(1 - xh).astype(BF)
        x_copy(s).start()
        XO[s] = half(xh)

    def slope(s):
        q = piece(s)
        x_copy(s).wait_recv()
        preact = XO[s] + XR[s].astype(F32)
        gate = jax.nn.sigmoid(preact)
        hidden = preact * gate
        cotangent = cot[rows(q * GRP, GRP), :].astype(F32)
        SL[s, rows(d * GRP, GRP)] = (cotangent * gate * (1.0 + preact * (1.0 - gate))).astype(BF)
        s_copy(s).start()
        square = hidden * hidden
        total = square[:, :128]
        for j in range(1, FC // 128):
            total += square[:, j * 128 : (j + 1) * 128]

        @pl.when(s == 0)
        def _():
            NR[f] = total

        @pl.when(s > 0)
        def _():
            NS[s] = total
            n_copy(s).start()

    def spread_z(s):
        s_copy(s).wait_recv()
        for dz in (2, 1, 3):
            z_copy(s, dz).start()

    def gradient(s):
        q = piece(s)
        for dz in (1, 3, 2):
            z_copy(s, dz).wait_recv()

        def tile(m, _):
            here = pl.ds(pl.multiple_of(m * 256, 256), 256)
            ACC[here, :] += lax.dot_general(
                T[q, :, here], SL[s], (((0,), (0,)), ((), ())), preferred_element_type=F32
            )
            return 0

        lax.fori_loop(0, TC // 256, tile, 0)

    def when_in(s, run):
        @pl.when((s >= 0) & (s < NF))
        def _():
            run(s)

    def stage(i, _):
        when_in(i, forward)
        when_in(i - LAG_X, reduce_z)
        when_in(i - LAG_S, slope)
        when_in(i - LAG_Z, spread_z)
        tokens_on(i + TOKEN_LEAD)

        @pl.when(i == FIRST_AT)
        def _():
            send_state(1, old_m, out_m)
            own_state(1, out_m).start()
            load_all(old_v)

        @pl.when(i == SECOND_AT)
        def _():
            send_state(2, old_v, out_v)
            own_state(2, out_v).start()

        when_in(i - LAG_G, gradient)
        return 0

    lax.fori_loop(0, NF + LAG_G, stage, 0)

    g_out = pltpu.make_async_copy(ACC, out_g, own_sem.at[4])
    g_out.start()

    def n_wait(s, total):
        n_landed(s).wait_recv()
        return total + NR[piece(s)]

    square = jnp.sum(lax.fori_loop(1, NF, n_wait, NR[f]), axis=1, keepdims=True)
    out_n[...] = jnp.broadcast_to(jnp.sqrt(square / FF + 1e-06), (GRP, 128))

    for copy in first_sends + second_sends:
        copy.wait_send()
    w_out.wait()
    own_state(1, out_m).wait()
    own_state(2, out_v).wait()

    def t1_end(k, _):
        t1_copy(k).wait_send()
        return 0

    lax.fori_loop(1, 8, t1_end, 0)

    def end(k, _):
        for i, dst in ((0, W), (1, out_m), (2, out_v)):
            state_copy(i, dst, k).wait_send()
        for i, dst in ((1, out_m), (2, out_v)):
            state_landed(i, dst, k).wait_recv()
        n_copy(k).wait_send()
        return 0

    lax.fori_loop(1, NF, end, 0)

    def end_stage(s, _):
        for dz in (1, 2, 3):
            rs_copy(s, dz).wait_send()
            z_copy(s, dz).wait_send()
        x_copy(s).wait_send()
        s_copy(s).wait_send()

        @pl.when((lax.rem(s, 2) == 0) & (s >= 4))
        def _():
            token_copy(piece(s), fw_send.at[s], sibling).wait_send()

        return 0

    lax.fori_loop(0, NF, end_stage, 0)
    g_out.wait()


def update_kernel(w, m, v, g, new_w, new_m, new_v):
    weight, grad = w[...].astype(F32), g[...] * SCALE
    first = 0.9 * m[...].astype(F32) + 0.1 * grad
    second = 0.95 * v[...].astype(F32) + 0.05 * grad * grad
    new_m[...] = first
    new_v[...] = second
    update = first / (1.0 - 0.9**10) / (jnp.sqrt(second / (1.0 - 0.95**10)) + 1e-08)
    new_w[...] = weight - 0.02 * (update + 0.1 * weight)


def body(old_weight, old_first, old_second, tokens, cotangent):
    anywhere = pl.BlockSpec(memory_space=pl.ANY)
    vmem = pl.BlockSpec(memory_space=pltpu.VMEM)
    tile = jax.ShapeDtypeStruct((TC, FC), BF)
    dma = pltpu.SemaphoreType.DMA
    w, m, v, g, n = pl.pallas_call(
        step_kernel,
        out_shape=(
            tile, tile, tile,
            jax.ShapeDtypeStruct((TC, FC), F32),
            jax.ShapeDtypeStruct((GRP, 128), F32),
        ),
        in_specs=[vmem, vmem, anywhere, anywhere, anywhere],
        out_specs=(anywhere, anywhere, anywhere, anywhere, vmem),
        scratch_shapes=[
            pltpu.VMEM((NF, 8 * GRP, TC), BF),
            pltpu.VMEM((TC, FC), BF),
            pltpu.VMEM((NF, 8 * GRP, FC), BF),
            pltpu.VMEM((3, NF, 64, FC), BF),
            pltpu.VMEM((NF, GRP, FC), F32),
            pltpu.VMEM((NF, GRP, FC), BF),
            pltpu.VMEM((NF, GRP, FC), BF),
            pltpu.VMEM((NF, 8 * GRP, FC), BF),
            pltpu.VMEM((TC, FC), F32),
            pltpu.VMEM((NF, SR, FC), F32),
            pltpu.VMEM((3, NF, SR, FC), BF),
            pltpu.VMEM((NF, GRP, 128), F32),
            pltpu.VMEM((NF, GRP, 128), F32),
            dma((NF,)), dma((3, NF)), dma((3, NF)), dma((5,)), dma((8,)), dma((8,)), dma((9,)), dma((NF,)), dma((NF,)),
            dma((3, NF)), dma((3, NF)), dma((NF,)), dma((NF,)), dma((NF,)), dma((NF,)),
            dma((3, NF)), dma((3, NF)), dma((NF,)), dma((NF,)),
        ],
        compiler_params=pltpu.CompilerParams(
            collective_id=1, has_side_effects=True, vmem_limit_bytes=60 << 20
        ),
        name="train_step",
    )(tokens, cotangent, old_weight, old_first, old_second)

    rows = 128
    block = pl.BlockSpec((rows, FC), lambda i: (i, 0))
    shape = jax.ShapeDtypeStruct((TC, FC), F32)
    new_weight, new_first, new_second = pl.pallas_call(
        update_kernel,
        grid=(TC // rows,),
        out_shape=(shape, shape, shape),
        in_specs=[block] * 4,
        out_specs=(block, block, block),
        name="adamw_update",
    )(w, m, v, g)
    return new_weight, new_first, new_second, n[:, 0]


def solution(mesh):
    placed = (
        P(("dp", "fsdp"), None),
        P(("dp", "fsdp"), None),
        P(("dp", "fsdp"), None),
        P(("dp", "fsdp"), None),
        P("dp", "fsdp"),
    )
    return jax.shard_map(
        body,
        mesh=mesh,
        in_specs=placed,
        out_specs=(P("dp", "fsdp"), P("dp", "fsdp"), P("dp", "fsdp"), P(("dp", "fsdp"))),
        check_vma=False,
    )
```

time: 516 us -> 240 us (0.47)
  waiting for transfers between devices: 333 us -> 0 us
  Pallas kernels: 0 us -> 237 us
  blocking collectives: 72.5 us -> 0 us
  matrix products: 31.7 us -> 0 us
  local copies, waits for them, and re-layouts: 32 us -> 1.34 us
  other arithmetic: 22.4 us -> 0 us
  between operations: 14.5 us -> 0.64 us
  starting transfers between devices: 9.01 us -> 0 us
    pallas_call x0 -> x2, Pallas kernels: none -> 237 us  [the longest x1 226 us: body(): pl.pallas_call(step_kernel, out_shape=(tile, tile, tile, jax.ShapeDtypeSt...]
    all_gather x2 -> x0, waiting for transfers between devices: 192 us -> none  [the longest x1 168 us: body(): lax.all_gather(weight_low, 'dp', axis=0, tiled=True)]
    reduce_scatter x1 -> x0, waiting for transfers between devices: 72.6 us -> none  [body(): lax.psum_scatter((lax.dot_general(token_cols, slope, (((0,), (0,)), ((),...]
    all_to_all x2 -> x0, waiting for transfers between devices: 67.5 us -> none  [the longest x1 38.6 us: body(): lax.all_to_all(old_first.astype(jnp.bfloat16), 'fsdp', split_axis=1, conc...]
    all_to_all x1 -> x0, blocking collectives: 44.9 us -> none  [body(): lax.all_to_all(old_weight.astype(jnp.bfloat16), 'fsdp', split_axis=1, con...]
    dot_general x2 -> x0, matrix products: 31.7 us -> none  [the longest x1 19.7 us: body(): jnp.dot(token_cols, lax.all_gather(weight_low, 'dp', axis=0, tiled=True),...]
    unnamed x1 -> x0, blocking collectives: 27.7 us -> none
    unnamed x14 -> x0, local copies, waits for them, and re-layouts: 15.6 us -> none
  transfers between devices with their start and end apart: 5 -> 0, of which waited for: 5 -> 0; matrix products, arithmetic and copies ran while one was open for 6% -> 0% of each run, Pallas kernels for 0% -> 0%
where the time goes in v1:
time: 240 us; the launch traced here: 239 us
  Pallas kernels  237 us (99%)
    pallas_call x1, Pallas kernels, body(): pl.pallas_call(step_kernel, out_shape=(tile, tile, tile, jax.ShapeDtypeSt...  226 us
    pallas_call x1, Pallas kernels, body(): pl.pallas_call(update_kernel, grid=(TC // rows,), out_shape=(shape, shape...  11.1 us

profile of v1, /device:TPU:0, one launch (start us, length us, event | category | flops | bytes accessed | tf_op | source)
XLA Modules:
  0.0 238.6 jit_solution(13778713703408671054)
XLA Ops:
  0.6 225.6 %train_step.1 = (bf16[1024,896]{1,0:T(8,128)(2,1)}, bf16[1024,896]{1,0:T(8,128)(2,1)}, bf16[1024,896]{1,0:T(8,128)(2,1)}, f32[1024,896]{1,0:T(8,128)}, f32[32,128]{1,0:T(8,128)}) custom-call(bf16[32,8192]{1,0:T(8,128)(2,1)} %tok.1, bf16[512,896]{1,0:T(8,128)(2,1)} %cot.1, f32[64,14336]{1,0:T(8,128)} %old_w.1, f32[64,14336]{1,0:T(8,128)} %old_m.1, ...), custom_call_target="tpu_custom_call" | custom-call | tf_op jit(solution)/shard_map/train_step/pallas_call | solution.py:360
  226.2 1.3 slice_reduce_fusion
  227.6 11.1 %adamw_update.1 = (f32[1024,896]{1,0:T(8,128)}, f32[1024,896]{1,0:T(8,128)}, f32[1024,896]{1,0:T(8,128)}) custom-call(bf16[1024,896]{1,0:T(8,128)(2,1)} %get-tuple-element.12.w, bf16[1024,896]{1,0:T(8,128)(2,1)} %get-tuple-element.13.m, bf16[1024,896]{1,0:T(8,128)(2,1)} %get-tuple-element.14.v, f32[1024,896]{1,0:T(8,128)} %get-tuple-element.15.g), custom_call_target="tpu_custom_call" | custom-call | tf_op jit(solution)/shard_map/adamw_update/pallas_call | solution.py:396

commit v2 on v1

--- a/solution.py
+++ b/solution.py
@@ -12,13 +12,15 @@
 SCALE = D ** (-0.5)
 NF = 16
 NZ = 4
+UPD_ROWS = 256
 GRP = 32
 TC = 1024
 FC = 896
 SR = 64
 TOKEN_LEAD = 2
-LAG_X, LAG_S, LAG_Z, LAG_G = 2, 3, 4, 6
-FIRST_AT, SECOND_AT = 2, 5
+LAGS = (1, 2, 3, 4, 5, 7)
+LAG_M, LAG_X, LAG_S, LAG_Z, LAG_H, LAG_G = LAGS
+STATES_AT = 6
 MESH = pl.DeviceIdType.MESH
 BF, F32 = jnp.bfloat16, jnp.float32
 
@@ -26,9 +28,9 @@
 def step_kernel(
     tok, cot, old_w, old_m, old_v,
     out_w, out_m, out_v, out_g, out_n,
-    T, W, PS, RR, XO, XS, XR, SL, ACC, ST, CB, NS, NR,
+    T, W, PS, TR, RR, XO, XS, XR, SL, ACC, ST, CB, NS, NR,
     ld_sem, st_send, st_recv, own_sem, t1_send, t1_recv, tk_send, fw_send, tk_recv,
-    rs_send, rs_recv, x_send, x_recv, s_send, s_recv, z_send, z_recv, n_send, n_recv,
+    tr_send, tr_recv, rs_send, rs_recv, x_send, x_recv, s_send, s_recv, z_send, z_recv, n_send, n_recv,
 ):
     d, f = lax.axis_index("dp"), lax.axis_index("fsdp")
     z, xh = lax.div(d, 2), lax.rem(d, 2)
@@ -38,7 +40,12 @@
         return lax.rem(y + dy, 4) * 4 + lax.rem(xl + dxl, 2) * 2 + lax.rem(c + dc, 2)
 
     def piece(s):
-        return at_f(lax.div(s, 4), lax.rem(lax.div(s, 2), 2), lax.rem(s, 2))
+        far = lax.div(jnp.maximum(s - 4, 0), 6)
+        near = lax.div(lax.rem(jnp.maximum(s - 4, 0), 6), 2)
+        along = 1 + 2 * near - 3 * lax.div(near, 2)
+        dy = jnp.where(s < 4, 0, along)
+        dxl = jnp.where(s < 4, lax.div(s, 2), far)
+        return at_f(dy, dxl, lax.rem(s, 2))
 
     def at_d(dz, dxh):
         return lax.rem(z + dz, NZ) * 2 + lax.rem(xh + dxh, 2)
@@ -51,13 +58,13 @@
     def rows(start, size):
         return pl.ds(pl.multiple_of(start, 32), size)
 
-    def load(old, k):
+    def load(old, i, k):
         cols = pl.ds(pl.multiple_of(piece(k) * FC, 128), FC)
-        return pltpu.make_async_copy(old.at[:, cols], ST.at[k], ld_sem.at[k])
-
-    def load_all(old):
-        def go(k, _):
-            load(old, k).start()
+        return pltpu.make_async_copy(old.at[:, cols], ST.at[i % 2, k], ld_sem.at[i % 2, k])
+
+    def load_all(old, i):
+        def go(n, _):
+            load(old, i, NF - 1 - n).start()
             return 0
 
         lax.fori_loop(0, NF, go, 0)
@@ -71,24 +78,23 @@
         q = piece(k)
         return remote(CB.at[i, k], dst.at[rows(q * SR, SR)], st_send.at[i, k], st_recv.at[i, q], (d, q))
 
-    def send_state(i, old, dst):
-        def go(n, _):
-            k = NF - 1 - n
-            load(old, k).wait()
-            CB[i, k] = ST[k].astype(BF)
-
-            @pl.when(k > 0)
-            def _():
-                state_copy(i, dst, k).start()
-
-            return 0
-
-        lax.fori_loop(0, NF, go, 0)
+    def send_state(i, old, dst, k):
+        load(old, i, k).wait()
+        CB[i, k] = ST[i % 2, k].astype(BF)
+
+        @pl.when(k > 0)
+        def _():
+            state_copy(i, dst, k).start()
+
+        @pl.when(k == 0)
+        def _():
+            own_state(i, dst).start()
 
     def own_state(i, dst):
         return pltpu.make_async_copy(CB.at[i, 0], dst.at[rows(f * SR, SR)], own_sem.at[i])
 
-    load_all(old_w)
+    load_all(old_w, 0)
+    load_all(old_m, 1)
 
     barrier = pltpu.get_barrier_semaphore()
 
@@ -125,9 +131,12 @@
     lax.fori_loop(1, 8, t1_go, 0)
     T[f, rows(d * GRP, GRP)] = tok[:, pl.ds(pl.multiple_of(d * TC, 128), TC)]
 
-    send_state(0, old_w, W)
-    own_state(0, W).start()
-    load_all(old_m)
+    def w_go(n, _):
+        send_state(0, old_w, W, NF - 1 - n)
+        return 0
+
+    lax.fori_loop(0, NF, w_go, 0)
+    load_all(old_v, 2)
 
     def t1_wait(k, _):
         t1_landed(k).wait_recv()
@@ -166,12 +175,19 @@
 
     ACC[...] = jnp.zeros_like(ACC)
 
-    def rs_copy(s, dz):
-        zz = lax.rem(z + dz, NZ)
-        return remote(
-            PS.at[s, rows(zz * 64, 64)], RR.at[dz - 1, s], rs_send.at[dz - 1, s], rs_recv.at[dz - 1, s],
-            (at_d(dz, 0), f),
-        )
+    def to_z(way):
+        return (at_d((1, 3)[way], 0), f)
+
+    def block_z(dz):
+        return lax.rem(z + dz, NZ) * 64
+
+    def transit(s, way):
+        here = rows(block_z(2) + way * GRP, GRP)
+        return remote(PS.at[s, here], TR.at[way, s], tr_send.at[way, s], tr_recv.at[way, s], to_z(way))
+
+    def rs_copy(s, way):
+        here = rows(block_z((1, 3)[way]), 64)
+        return remote(PS.at[s, here], RR.at[way, s], rs_send.at[way, s], rs_recv.at[way, s], to_z(way))
 
     def x_copy(s):
         return remote(XS.at[s], XR.at[s], x_send.at[s], x_recv.at[s], (at_d(0, 1), f))
@@ -180,9 +196,13 @@
         mine = SL.at[s, rows(d * GRP, GRP)]
         return remote(mine, mine, s_send.at[s], s_recv.at[s], (at_d(0, 1), f))
 
-    def z_copy(s, dz):
+    def z_copy(s, way):
         mine = SL.at[s, rows(z * 64, 64)]
-        return remote(mine, mine, z_send.at[dz - 1, s], z_recv.at[dz - 1, s], (at_d(dz, 0), f))
+        return remote(mine, mine, z_send.at[way, s], z_recv.at[way, s], to_z(way))
+
+    def z_on(s, way):
+        here = SL.at[s, rows(block_z((3, 1)[way]) + way * GRP, GRP)]
+        return remote(here, here, z_send.at[2 + way, s], z_recv.at[2 + way, s], to_z(way))
 
     def n_copy(s):
         return remote(NS.at[s], NR.at[f], n_send.at[s], n_recv.at[f], (d, piece(s)))
@@ -207,17 +227,24 @@
 
         part = jnp.dot(T[q], W[...], preferred_element_type=F32) * SCALE
         PS[s] = part.astype(BF)
-        for dz in (2, 1, 3):
-            rs_copy(s, dz).start()
+        for way in (0, 1):
+            transit(s, way).start()
+
+    def merge(s):
+        for way in (0, 1):
+            transit(s, way).wait_recv()
+            here = rows(block_z((1, 3)[way]) + way * GRP, GRP)
+            PS[s, here] = (PS[s, here].astype(F32) + TR[way, s].astype(F32)).astype(BF)
+            rs_copy(s, way).start()
 
     def reduce_z(s):
-        for dz in (1, 3, 2):
-            rs_copy(s, dz).wait_recv()
+        for way in (0, 1):
+            rs_copy(s, way).wait_recv()
 
         def half(h):
             own = PS[s, rows(z * 64 + h * GRP, GRP)].astype(F32)
             here = rows(h * GRP, GRP)
-            return own + RR[0, s, here].astype(F32) + RR[1, s, here].astype(F32) + RR[2, s, here].astype(F32)
+            return own + RR[0, s, here].astype(F32) + RR[1, s, here].astype(F32)
 
         XS[s] = half(1 - xh).astype(BF)
         x_copy(s).start()
@@ -248,13 +275,18 @@
 
     def spread_z(s):
         s_copy(s).wait_recv()
-        for dz in (2, 1, 3):
-            z_copy(s, dz).start()
+        for way in (0, 1):
+            z_copy(s, way).start()
+
+    def hand_on(s):
+        for way in (0, 1):
+            z_copy(s, way).wait_recv()
+            z_on(s, way).start()
 
     def gradient(s):
         q = piece(s)
-        for dz in (1, 3, 2):
-            z_copy(s, dz).wait_recv()
+        for way in (0, 1):
+            z_on(s, way).wait_recv()
 
         def tile(m, _):
             here = pl.ds(pl.multiple_of(m * 256, 256), 256)
@@ -272,21 +304,19 @@
 
     def stage(i, _):
         when_in(i, forward)
+        when_in(i - LAG_M, merge)
         when_in(i - LAG_X, reduce_z)
         when_in(i - LAG_S, slope)
         when_in(i - LAG_Z, spread_z)
+        when_in(i - LAG_H, hand_on)
         tokens_on(i + TOKEN_LEAD)
 
-        @pl.when(i == FIRST_AT)
-        def _():
-            send_state(1, old_m, out_m)
-            own_state(1, out_m).start()
-            load_all(old_v)
-
-        @pl.when(i == SECOND_AT)
-        def _():
-            send_state(2, old_v, out_v)
-            own_state(2, out_v).start()
+        k = NF - 1 - (i - STATES_AT)
+
+        @pl.when((k >= 0) & (k < NF))
+        def _():
+            send_state(1, old_m, out_m, k)
+            send_state(2, old_v, out_v, k)
 
         when_in(i - LAG_G, gradient)
         return 0
@@ -326,9 +356,11 @@
     lax.fori_loop(1, NF, end, 0)
 
     def end_stage(s, _):
-        for dz in (1, 2, 3):
-            rs_copy(s, dz).wait_send()
-            z_copy(s, dz).wait_send()
+        for way in (0, 1):
+            transit(s, way).wait_send()
+            rs_copy(s, way).wait_send()
+            z_copy(s, way).wait_send()
+            z_on(s, way).wait_send()
         x_copy(s).wait_send()
         s_copy(s).wait_send()
 
@@ -348,7 +380,7 @@
     second = 0.95 * v[...].astype(F32) + 0.05 * grad * grad
     new_m[...] = first
     new_v[...] = second
-    update = first / (1.0 - 0.9**10) / (jnp.sqrt(second / (1.0 - 0.95**10)) + 1e-08)
+    update = first * (1.0 / (1.0 - 0.9**10)) / (jnp.sqrt(second * (1.0 / (1.0 - 0.95**10))) + 1e-08)
     new_w[...] = weight - 0.02 * (update + 0.1 * weight)
 
 
@@ -370,19 +402,20 @@
             pltpu.VMEM((NF, 8 * GRP, TC), BF),
             pltpu.VMEM((TC, FC), BF),
             pltpu.VMEM((NF, 8 * GRP, FC), BF),
-            pltpu.VMEM((3, NF, 64, FC), BF),
+            pltpu.VMEM((2, NF, GRP, FC), BF),
+            pltpu.VMEM((2, NF, 64, FC), BF),
             pltpu.VMEM((NF, GRP, FC), F32),
             pltpu.VMEM((NF, GRP, FC), BF),
             pltpu.VMEM((NF, GRP, FC), BF),
             pltpu.VMEM((NF, 8 * GRP, FC), BF),
             pltpu.VMEM((TC, FC), F32),
-            pltpu.VMEM((NF, SR, FC), F32),
+            pltpu.VMEM((2, NF, SR, FC), F32),
             pltpu.VMEM((3, NF, SR, FC), BF),
             pltpu.VMEM((NF, GRP, 128), F32),
             pltpu.VMEM((NF, GRP, 128), F32),
-            dma((NF,)), dma((3, NF)), dma((3, NF)), dma((5,)), dma((8,)), dma((8,)), dma((9,)), dma((NF,)), dma((NF,)),
-            dma((3, NF)), dma((3, NF)), dma((NF,)), dma((NF,)), dma((NF,)), dma((NF,)),
-            dma((3, NF)), dma((3, NF)), dma((NF,)), dma((NF,)),
+            dma((2, NF)), dma((3, NF)), dma((3, NF)), dma((5,)), dma((8,)), dma((8,)), dma((9,)), dma((NF,)), dma((NF,)),
+            dma((2, NF)), dma((2, NF)), dma((2, NF)), dma((2, NF)), dma((NF,)), dma((NF,)), dma((NF,)), dma((NF,)),
+            dma((4, NF)), dma((4, NF)), dma((NF,)), dma((NF,)),
         ],
         compiler_params=pltpu.CompilerParams(
             collective_id=1, has_side_effects=True, vmem_limit_bytes=60 << 20
@@ -390,7 +423,7 @@
         name="train_step",
     )(tokens, cotangent, old_weight, old_first, old_second)
 
-    rows = 128
+    rows = UPD_ROWS
     block = pl.BlockSpec((rows, FC), lambda i: (i, 0))
     shape = jax.ShapeDtypeStruct((TC, FC), F32)
     new_weight, new_first, new_second = pl.pallas_call(

time: 240 us -> 192 us (0.80)
  Pallas kernels: 237 us -> 190 us
    pallas_call x1, Pallas kernels: 226 us -> 181 us  [body(): pl.pallas_call(step_kernel, out_shape=(tile, tile, tile, jax.ShapeDtypeSt...]
where the time goes in v2:
time: 192 us
  Pallas kernels  190 us (99%)
    pallas_call x1, Pallas kernels, body(): pl.pallas_call(step_kernel, out_shape=(tile, tile, tile, jax.ShapeDtypeSt...  181 us
    pallas_call x1, Pallas kernels, body(): pl.pallas_call(update_kernel, grid=(TC // rows,), out_shape=(shape, shape...  8.9 us

profile of v2, /device:TPU:0, one launch (start us, length us, event | category | flops | bytes accessed | tf_op | source)
XLA Modules:
  0.0 192.2 jit_solution(4103905269071000373)
XLA Ops:
  0.6 181.3 %train_step.1 = (bf16[1024,896]{1,0:T(8,128)(2,1)}, bf16[1024,896]{1,0:T(8,128)(2,1)}, bf16[1024,896]{1,0:T(8,128)(2,1)}, f32[1024,896]{1,0:T(8,128)}, f32[32,128]{1,0:T(8,128)}) custom-call(bf16[32,8192]{1,0:T(8,128)(2,1)} %tok.1, bf16[512,896]{1,0:T(8,128)(2,1)} %cot.1, f32[64,14336]{1,0:T(8,128)} %old_w.1, f32[64,14336]{1,0:T(8,128)} %old_m.1, ...), custom_call_target="tpu_custom_call" | custom-call | tf_op jit(solution)/shard_map/train_step/pallas_call | solution.py:392
  182.0 1.3 slice_reduce_fusion
  183.3 8.9 %adamw_update.1 = (f32[1024,896]{1,0:T(8,128)}, f32[1024,896]{1,0:T(8,128)}, f32[1024,896]{1,0:T(8,128)}) custom-call(bf16[1024,896]{1,0:T(8,128)(2,1)} %get-tuple-element.12.w, bf16[1024,896]{1,0:T(8,128)(2,1)} %get-tuple-element.13.m, bf16[1024,896]{1,0:T(8,128)(2,1)} %get-tuple-element.14.v, f32[1024,896]{1,0:T(8,128)} %get-tuple-element.15.g), custom_call_target="tpu_custom_call" | custom-call | tf_op jit(solution)/shard_map/adamw_update/pallas_call | solution.py:429

commit v3 on v2

v3 whole, which is shorter than its diff:
```python
import functools

import jax
import jax.numpy as jnp
from jax import lax
from jax.experimental import pallas as pl
from jax.experimental.pallas import tpu as pltpu
from jax.sharding import PartitionSpec as P

D = 8192
FF = 14336
SCALE = D ** (-0.5)
NF = 16
NZ = 4
UPD_ROWS = 512
UPD_LIMIT = 60 << 20
GRP = 32
TC = 1024
FC = 896
SR = 64
GROUPS = ((0, 512), (512, 384), (0, 896))
SPLIT = 4
STEPS = NF + SPLIT
TOKEN_LEAD = 2
LAGS = (1, 2, 3, 4, 5, 7)
LAG_M, LAG_X, LAG_S, LAG_Z, LAG_H, LAG_G = LAGS
STATES_AT = 5
MESH = pl.DeviceIdType.MESH
BF, F32 = jnp.bfloat16, jnp.float32


def step_kernel(
    tok, cot, old_w, old_m, old_v,
    out_w, out_m, out_v, out_g, out_n,
    T, W, PS, TR, RR, XO, XS, XR, SL, ACC, ST, CB, NS, NR, COT,
    ld_sem, own_sem, sent, got, tk_recv, tr_recv, rs_recv, x_recv, s_recv, z_recv, on_recv,
):
    d, f = lax.axis_index("dp"), lax.axis_index("fsdp")
    z, xh = lax.div(d, 2), lax.rem(d, 2)
    y, xl, c = lax.div(f, 4), lax.rem(lax.div(f, 2), 2), lax.rem(f, 2)

    def at_f(dy, dxl, dc):
        return lax.rem(y + dy, 4) * 4 + lax.rem(xl + dxl, 2) * 2 + lax.rem(c + dc, 2)

    def piece(s):
        far = lax.div(jnp.maximum(s - 4, 0), 6)
        near = lax.div(lax.rem(jnp.maximum(s - 4, 0), 6), 2)
        along = 1 + 2 * near - 3 * lax.div(near, 2)
        dy = jnp.where(s < 4, 0, along)
        dxl = jnp.where(s < 4, lax.div(s, 2), far)
        return at_f(dy, dxl, lax.rem(s, 2))

    def at_d(dz, dxh):
        return lax.rem(z + dz, NZ) * 2 + lax.rem(xh + dxh, 2)

    def remote(src, dst, send, recv, dev):
        return pltpu.make_async_remote_copy(
            src_ref=src, dst_ref=dst, send_sem=send, recv_sem=recv, device_id=dev, device_id_type=MESH
        )

    def drain(ref, sem):
        pltpu.make_async_copy(ref, ref, sem).wait()

    def rows(start, size):
        return pl.ds(pl.multiple_of(start, 32), size)

    def load(old, i, k):
        cols = pl.ds(pl.multiple_of(piece(k) * FC, 128), FC)
        return pltpu.make_async_copy(old.at[:, cols], ST.at[i % 2, k], ld_sem.at[i])

    def load_all(old, i):
        def go(k, _):
            load(old, i, k).start()
            return 0

        lax.fori_loop(0, NF, go, 0)

    def state_copy(i, dst, k):
        return remote(
            CB.at[i, k], dst.at[rows(f * SR, SR)], sent.at[i], got.at[i], (d, piece(k))
        )

    def w_copy(g, k):
        cols = pl.ds(*GROUPS[g])
        return remote(
            CB.at[0, k, :, cols], W.at[rows(f * SR, SR), cols], sent.at[3 * g], got.at[3 * g], (d, piece(k))
        )

    def w_wait(g):
        drain(W.at[pl.ds(0, (NF - 1) * SR), pl.ds(*GROUPS[g])], got.at[3 * g])

    def state_wait(i, dst):
        drain(dst.at[pl.ds(0, (NF - 1) * SR)], got.at[i])

    def send_state(i, old, dst, k):
        CB[i, k] = ST[i % 2, k].astype(BF)

        @pl.when(k > 0)
        def _():
            state_copy(i, dst, k).start()

        @pl.when(k == 0)
        def _():
            own_state(i, dst).start()

    def own_state(i, dst):
        return pltpu.make_async_copy(CB.at[i, 0], dst.at[rows(f * SR, SR)], own_sem.at[i])

    load_all(old_w, 0)
    own_tokens = pltpu.make_async_copy(
        tok.at[:, pl.ds(pl.multiple_of(d * TC, 128), TC)], T.at[f, rows(d * GRP, GRP)], own_sem.at[0]
    )
    own_tokens.start()
    cot_load = pltpu.make_async_copy(cot, COT, own_sem.at[5])
    cot_load.start()
    load_all(old_m, 1)

    barrier = pltpu.get_barrier_semaphore()

    def greet_f(k, _):
        pl.semaphore_signal(barrier, inc=1, device_id=(d, piece(k)), device_id_type=MESH)
        return 0

    lax.fori_loop(1, NF, greet_f, 0)

    def greet_d(k, _):
        pl.semaphore_signal(barrier, inc=1, device_id=(lax.rem(d + k, 8), f), device_id_type=MESH)
        return 0

    lax.fori_loop(1, 8, greet_d, 0)
    pl.semaphore_wait(barrier, NF - 1 + 7)

    def t1_copy(k):
        q = lax.rem(d + k, 8)
        cols = pl.ds(pl.multiple_of(q * TC, 128), TC)
        return remote(
            tok.at[:, cols], T.at[f, rows(d * GRP, GRP)], sent.at[4], got.at[4], (q, f)
        )

    def t1_go(k, _):
        t1_copy(k).start()
        return 0

    lax.fori_loop(1, 8, t1_go, 0)

    drain(ST.at[0], ld_sem.at[0])

    def w_go(n, _):
        k = NF - 1 - n
        CB[0, k] = ST[0, k].astype(BF)

        @pl.when(k > 0)
        def _():
            w_copy(0, k).start()

        return 0

    lax.fori_loop(0, NF, w_go, 0)
    W[rows(f * SR, SR)] = CB[0, 0]
    load_all(old_v, 2)

    drain(T.at[0, pl.ds(0, 7 * GRP)], got.at[4])
    own_tokens.wait()

    def token_copy(q, dev_f, kind=5):
        return remote(T.at[q], T.at[q], sent.at[kind], tk_recv.at[q], (d, dev_f))

    def landed(q):
        return pltpu.make_async_copy(T.at[q], T.at[q], tk_recv.at[q])

    sibling = at_f(0, 0, 1)
    partner = at_f(0, 1, 0)
    early_sends = [token_copy(f, partner), token_copy(f, sibling)]
    first_sends = [token_copy(f, at_f(dy, 0, 0)) for dy in (1, 3)]
    second_sends = [token_copy(partner, at_f(dy, 0, 0)) for dy in (1, 3)]
    second_sends += [token_copy(partner, sibling)]

    def y_on(dxl):
        return token_copy(at_f(3 - 2 * c, dxl, 0), at_f(1 + 2 * c, 0, 0))

    for copy in early_sends:
        copy.start()
    ACC[...] = jnp.zeros_like(ACC)
    cot_load.wait()
    w_wait(0)

    def w_rest(n, _):
        w_copy(1, NF - 1 - n).start()
        return 0

    lax.fori_loop(0, NF - 1, w_rest, 0)
    for copy in first_sends:
        copy.start()
    w_out = pltpu.make_async_copy(W, out_w, own_sem.at[3])

    def to_z(way):
        return (at_d((1, 3)[way], 0), f)

    def block_z(dz):
        return lax.rem(z + dz, NZ) * 64

    def step_of(g, s):
        return s if g == 0 else s + SPLIT

    def transit(g, s, way):
        here, cols = rows(block_z(2) + way * GRP, GRP), pl.ds(*GROUPS[g])
        return remote(
            PS.at[s, here, cols], TR.at[way, s, :, cols], sent.at[7], tr_recv.at[step_of(g, s)], to_z(way)
        )

    def rs_copy(g, s, way):
        here, cols = rows(block_z((1, 3)[way]), 64), pl.ds(*GROUPS[g])
        return remote(
            PS.at[s, here, cols], RR.at[way, s, :, cols], sent.at[8], rs_recv.at[step_of(g, s)], to_z(way)
        )

    def x_copy(g, s):
        cols = pl.ds(*GROUPS[g])
        return remote(XS.at[s, :, cols], XR.at[s, :, cols], sent.at[9], x_recv.at[step_of(g, s)], (at_d(0, 1), f))

    def s_copy(g, s):
        mine = SL.at[s, rows(d * GRP, GRP), pl.ds(*GROUPS[g])]
        return remote(mine, mine, sent.at[10], s_recv.at[step_of(g, s)], (at_d(0, 1), f))

    def z_copy(g, s, way):
        mine = SL.at[s, rows(z * 64, 64), pl.ds(*GROUPS[g])]
        return remote(mine, mine, sent.at[11], z_recv.at[step_of(g, s)], to_z(way))

    def z_on(g, s, way):
        here = SL.at[s, rows(block_z((3, 1)[way]) + way * GRP, GRP), pl.ds(*GROUPS[g])]
        return remote(here, here, sent.at[12], on_recv.at[step_of(g, s)], to_z(way))

    def n_copy(s):
        return remote(NS.at[s], NR.at[f], sent.at[13], got.at[5], (d, piece(s)))

    def tokens_on(j):
        @pl.when((lax.rem(j, 2) == 0) & (j >= 4) & (j < NF))
        def _():
            q = piece(j)
            landed(q).wait()
            token_copy(q, sibling, 6).start()

        @pl.when(j == 6)
        def _():
            y_on(0).start()

        @pl.when(j == 12)
        def _():
            y_on(1).start()

    def forward(g, s):
        q, cols = piece(s), pl.ds(*GROUPS[g])

        if g != 1:

            @pl.when(lax.rem(s, 2) == 1)
            def _():
                landed(q).wait()
        if g == 1 or SPLIT == 0:

            @pl.when(s == 0)
            def _():
                w_wait(1)
                w_out.start()

        part = jnp.dot(T[q], W[:, cols], preferred_element_type=F32) * SCALE
        PS[s, :, cols] = part.astype(BF)
        for way in (0, 1):
            transit(g, s, way).start()

    def merge(g, s):
        cols = pl.ds(*GROUPS[g])
        drain(TR.at[:, s, :, cols], tr_recv.at[step_of(g, s)])
        for way in (0, 1):
            here = rows(block_z((1, 3)[way]) + way * GRP, GRP)
            PS[s, here, cols] = (PS[s, here, cols].astype(F32) + TR[way, s, :, cols].astype(F32)).astype(BF)
            rs_copy(g, s, way).start()

    def reduce_z(g, s):
        cols = pl.ds(*GROUPS[g])
        drain(RR.at[:, s, :, cols], rs_recv.at[step_of(g, s)])

        def half(h):
            own = PS[s, rows(z * 64 + h * GRP, GRP), cols].astype(F32)
            here = rows(h * GRP, GRP)
            return own + RR[0, s, here, cols].astype(F32) + RR[1, s, here, cols].astype(F32)

        XS[s, :, cols] = half(1 - xh).astype(BF)
        x_copy(g, s).start()
        XO[s, :, cols] = half(xh)

    def slope(g, s):
        q, cols = piece(s), pl.ds(*GROUPS[g])
        x_copy(g, s).wait_recv()
        preact = XO[s, :, cols] + XR[s, :, cols].astype(F32)
        gate = jax.nn.sigmoid(preact)
        hidden = preact * gate
        cotangent = COT[rows(q * GRP, GRP), cols].astype(F32)
        SL[s, rows(d * GRP, GRP), cols] = (cotangent * gate * (1.0 + preact * (1.0 - gate))).astype(BF)
        s_copy(g, s).start()
        square = hidden * hidden
        total = square[:, :128]
        for j in range(1, GROUPS[g][1] // 128):
            total += square[:, j * 128 : (j + 1) * 128]
        if g == 1:
            total += NS[s]
        NS[s] = total
        if g > 0:

            @pl.when(s == 0)
            def _():
                NR[f] = total

            @pl.when(s > 0)
            def _():
                n_copy(s).start()

    def spread_z(g, s):
        s_copy(g, s).wait_recv()
        for way in (0, 1):
            z_copy(g, s, way).start()

    def hand_on(g, s):
        drain(RR.at[:, s, :, pl.ds(*GROUPS[g])], z_recv.at[step_of(g, s)])
        for way in (0, 1):
            z_on(g, s, way).start()

    def gradient(g, s):
        q, cols = piece(s), pl.ds(*GROUPS[g])
        drain(TR.at[:, s, :, cols], on_recv.at[step_of(g, s)])

        def tile(m, _):
            here = pl.ds(pl.multiple_of(m * 256, 256), 256)
            ACC[here, cols] += lax.dot_general(
                T[q, :, here], SL[s, :, cols], (((0,), (0,)), ((), ())), preferred_element_type=F32
            )
            return 0

        lax.fori_loop(0, TC // 256, tile, 0)

    def when_in(i, run):
        for g, first, last, less in ((0, 0, SPLIT, 0), (1, SPLIT, 2 * SPLIT, SPLIT), (2, 2 * SPLIT, STEPS, SPLIT)):

            @pl.when((i >= first) & (i < last))
            def _():
                run(g, i - less)

    def stage(i, _):
        when_in(i, forward)
        when_in(i - LAG_M, merge)
        when_in(i - LAG_X, reduce_z)
        when_in(i - LAG_S, slope)
        when_in(i - LAG_Z, spread_z)
        when_in(i - LAG_H, hand_on)
        tokens_on(i - SPLIT + TOKEN_LEAD)

        @pl.when(i == 0)
        def _():
            landed(partner).wait()
            for copy in second_sends:
                copy.start()

        @pl.when(i == STATES_AT)
        def _():
            drain(ST.at[1], ld_sem.at[1])
            drain(ST.at[0], ld_sem.at[2])

        @pl.when((i >= STATES_AT) & (i < STATES_AT + NF))
        def _():
            n = i - STATES_AT
            for u, old, dst in ((1, old_m, out_m), (2, old_v, out_v)):
                dy, dxl, dc = lax.rem(n + 2 * u + c, 4), lax.rem(lax.div(n, 4) + u, 2), lax.div(n, 8)
                near = jnp.where(dy == 1, 0, jnp.where(dy == 3, 1, 2))
                send_state(u, old, dst, jnp.where(dy == 0, 0, 4 + 4 * dxl + 2 * near) + 2 * dxl + dc)

        when_in(i - LAG_G, gradient)
        return 0

    lax.fori_loop(0, STEPS + LAG_G, stage, 0)

    g_out = pltpu.make_async_copy(ACC, out_g, own_sem.at[4])
    g_out.start()

    drain(NR.at[pl.ds(0, NF - 1)], got.at[5])
    square = jnp.sum(jnp.sum(NR[...], axis=0), axis=1, keepdims=True)
    out_n[...] = jnp.broadcast_to(jnp.sqrt(square / FF + 1e-06), (GRP, 128))

    w_out.wait()
    own_state(1, out_m).wait()
    own_state(2, out_v).wait()
    state_wait(1, out_m)
    state_wait(2, out_v)
    others = pl.ds(0, NF - 1)
    drain(CB.at[0, others, :, pl.ds(*GROUPS[0])], sent.at[0])
    drain(CB.at[1, others], sent.at[1])
    drain(CB.at[2, others], sent.at[2])
    drain(CB.at[0, others, :, pl.ds(*GROUPS[1])], sent.at[3])
    drain(T.at[0, pl.ds(0, 7 * GRP)], sent.at[4])
    drain(T.at[pl.ds(0, 9)], sent.at[5])
    drain(T.at[pl.ds(0, 6)], sent.at[6])
    drain(TR, sent.at[7])
    drain(RR, sent.at[8])
    drain(XS, sent.at[9])
    drain(XS, sent.at[10])
    drain(RR, sent.at[11])
    drain(TR, sent.at[12])
    drain(NS.at[others], sent.at[13])
    g_out.wait()


def update_kernel(w, m, v, g, new_w, new_m, new_v):
    weight, grad = w[...].astype(F32), g[...] * SCALE
    first = 0.9 * m[...].astype(F32) + 0.1 * grad
    second = 0.95 * v[...].astype(F32) + 0.05 * grad * grad
    new_m[...] = first
    new_v[...] = second
    update = first * (1.0 / (1.0 - 0.9**10)) / (jnp.sqrt(second * (1.0 / (1.0 - 0.95**10))) + 1e-08)
    new_w[...] = weight - 0.02 * (update + 0.1 * weight)


def body(old_weight, old_first, old_second, tokens, cotangent):
    anywhere = pl.BlockSpec(memory_space=pl.ANY)
    vmem = pl.BlockSpec(memory_space=pltpu.VMEM)
    tile = jax.ShapeDtypeStruct((TC, FC), BF)
    dma = pltpu.SemaphoreType.DMA
    w, m, v, g, n = pl.pallas_call(
        step_kernel,
        out_shape=(
            tile, tile, tile,
            jax.ShapeDtypeStruct((TC, FC), F32),
            jax.ShapeDtypeStruct((GRP, 128), F32),
        ),
        in_specs=[anywhere] * 5,
        out_specs=(anywhere, anywhere, anywhere, anywhere, vmem),
        scratch_shapes=[
            pltpu.VMEM((NF, 8 * GRP, TC), BF),
            pltpu.VMEM((TC, FC), BF),
            pltpu.VMEM((NF, 8 * GRP, FC), BF),
            pltpu.VMEM((2, NF, GRP, FC), BF),
            pltpu.VMEM((2, NF, 64, FC), BF),
            pltpu.VMEM((NF, GRP, FC), F32),
            pltpu.VMEM((NF, GRP, FC), BF),
            pltpu.VMEM((NF, GRP, FC), BF),
            pltpu.VMEM((NF, 8 * GRP, FC), BF),
            pltpu.VMEM((TC, FC), F32),
            pltpu.VMEM((2, NF, SR, FC), F32),
            pltpu.VMEM((3, NF, SR, FC), BF),
            pltpu.VMEM((NF, GRP, 128), F32),
            pltpu.VMEM((NF, GRP, 128), F32),
            pltpu.VMEM((8 * SR, FC), BF),
            dma((3,)), dma((6,)), dma((14,)), dma((6,)), dma((NF,)),
            dma((STEPS,)), dma((STEPS,)), dma((STEPS,)), dma((STEPS,)), dma((STEPS,)), dma((STEPS,)),
        ],
        compiler_params=pltpu.CompilerParams(
            collective_id=1, has_side_effects=True, vmem_limit_bytes=60 << 20
        ),
        name="train_step",
    )(tokens, cotangent, old_weight, old_first, old_second)

    rows = UPD_ROWS
    block = pl.BlockSpec((rows, FC), lambda i: (i, 0))
    shape = jax.ShapeDtypeStruct((TC, FC), F32)
    new_weight, new_first, new_second = pl.pallas_call(
        update_kernel,
        grid=(TC // rows,),
        out_shape=(shape, shape, shape),
        in_specs=[block] * 4,
        out_specs=(block, block, block),
        compiler_params=pltpu.CompilerParams(vmem_limit_bytes=UPD_LIMIT),
        name="adamw_update",
    )(w, m, v, g)
    return new_weight, new_first, new_second, n[:, 0]


def solution(mesh):
    placed = (
        P(("dp", "fsdp"), None),
        P(("dp", "fsdp"), None),
        P(("dp", "fsdp"), None),
        P(("dp", "fsdp"), None),
        P("dp", "fsdp"),
    )
    return jax.shard_map(
        body,
        mesh=mesh,
        in_specs=placed,
        out_specs=(P("dp", "fsdp"), P("dp", "fsdp"), P("dp", "fsdp"), P(("dp", "fsdp"))),
        check_vma=False,
    )
```

time: 192 us -> 182 us (0.948)
  Pallas kernels: 190 us -> 180 us
    pallas_call x1, Pallas kernels: 181 us -> 171 us  [body(): pl.pallas_call(step_kernel, out_shape=(tile, tile, tile, jax.ShapeDtypeSt...]
where the time goes in v3:
time: 182 us
  Pallas kernels  180 us (99%)
    pallas_call x1, Pallas kernels, body(): pl.pallas_call(step_kernel, out_shape=(tile, tile, tile, jax.ShapeDtypeSt...  171 us
    pallas_call x1, Pallas kernels, body(): pl.pallas_call(update_kernel, grid=(TC // rows,), out_shape=(shape, shape...  8.19 us

profile of v3, /device:TPU:0, one launch (start us, length us, event | category | flops | bytes accessed | tf_op | source)
XLA Modules:
  0.0 181.6 jit_solution(12715263732114016923)
XLA Ops:
  0.6 171.5 %train_step.1 = (bf16[1024,896]{1,0:T(8,128)(2,1)}, bf16[1024,896]{1,0:T(8,128)(2,1)}, bf16[1024,896]{1,0:T(8,128)(2,1)}, f32[1024,896]{1,0:T(8,128)}, f32[32,128]{1,0:T(8,128)}) custom-call(bf16[32,8192]{1,0:T(8,128)(2,1)} %tok.1, bf16[512,896]{1,0:T(8,128)(2,1)} %cot.1, f32[64,14336]{1,0:T(8,128)} %old_w.1, f32[64,14336]{1,0:T(8,128)} %old_m.1, ...), custom_call_target="tpu_custom_call" | custom-call | tf_op jit(solution)/shard_map/train_step/pallas_call | solution.py:426
  172.1 1.3 slice_reduce_fusion
  173.5 8.2 %adamw_update.1 = (f32[1024,896]{1,0:T(8,128)}, f32[1024,896]{1,0:T(8,128)}, f32[1024,896]{1,0:T(8,128)}) custom-call(bf16[1024,896]{1,0:T(8,128)(2,1)} %get-tuple-element.12.w, bf16[1024,896]{1,0:T(8,128)(2,1)} %get-tuple-element.13.m, bf16[1024,896]{1,0:T(8,128)(2,1)} %get-tuple-element.14.v, f32[1024,896]{1,0:T(8,128)} %get-tuple-element.15.g), custom_call_target="tpu_custom_call" | custom-call | tf_op jit(solution)/shard_map/adamw_update/pallas_call | solution.py:463

commit v4 on v3

--- a/solution.py
+++ b/solution.py
@@ -18,9 +18,12 @@
 TC = 1024
 FC = 896
 SR = 64
-GROUPS = ((0, 512), (512, 384), (0, 896))
+GROUPS = ((0, 512), (512, 384), (0, 896), (0, 896))
 SPLIT = 4
 STEPS = NF + SPLIT
+B_SET = (4, 2)
+B_EVERY, B_AT = B_SET
+NB = len([s for s in range(SPLIT, NF) if s % B_EVERY == B_AT])
 TOKEN_LEAD = 2
 LAGS = (1, 2, 3, 4, 5, 7)
 LAG_M, LAG_X, LAG_S, LAG_Z, LAG_H, LAG_G = LAGS
@@ -32,7 +35,7 @@
 def step_kernel(
     tok, cot, old_w, old_m, old_v,
     out_w, out_m, out_v, out_g, out_n,
-    T, W, PS, TR, RR, XO, XS, XR, SL, ACC, ST, CB, NS, NR, COT,
+    T, W, PS, TR, RR, XO, XS, XR, XB, SL, ACC, ST, CB, NS, NR, COT,
     ld_sem, own_sem, sent, got, tk_recv, tr_recv, rs_recv, x_recv, s_recv, z_recv, on_recv,
 ):
     d, f = lax.axis_index("dp"), lax.axis_index("fsdp")
@@ -108,7 +111,7 @@
 
     load_all(old_w, 0)
     own_tokens = pltpu.make_async_copy(
-        tok.at[:, pl.ds(pl.multiple_of(d * TC, 128), TC)], T.at[f, rows(d * GRP, GRP)], own_sem.at[0]
+        tok.at[:, pl.ds(pl.multiple_of(d * TC, 128), TC)], T.at[f, xh, rows(z * GRP, GRP)], own_sem.at[0]
     )
     own_tokens.start()
     cot_load = pltpu.make_async_copy(cot, COT, own_sem.at[5])
@@ -134,7 +137,7 @@
         q = lax.rem(d + k, 8)
         cols = pl.ds(pl.multiple_of(q * TC, 128), TC)
         return remote(
-            tok.at[:, cols], T.at[f, rows(d * GRP, GRP)], sent.at[4], got.at[4], (q, f)
+            tok.at[:, cols], T.at[f, xh, rows(z * GRP, GRP)], sent.at[4], got.at[4], (q, f)
         )
 
     def t1_go(k, _):
@@ -159,7 +162,7 @@
     W[rows(f * SR, SR)] = CB[0, 0]
     load_all(old_v, 2)
 
-    drain(T.at[0, pl.ds(0, 7 * GRP)], got.at[4])
+    drain(T.at[0, :, pl.ds(0, 7 * GRP // 2)], got.at[4])
     own_tokens.wait()
 
     def token_copy(q, dev_f, kind=5):
@@ -197,21 +200,25 @@
         return (at_d((1, 3)[way], 0), f)
 
     def block_z(dz):
-        return lax.rem(z + dz, NZ) * 64
+        return rows(lax.rem(z + dz, NZ) * GRP, GRP)
+
+    def part_z(dz, way):
+        return pl.ds(pl.multiple_of(lax.rem(z + dz, NZ) * GRP + way * 16, 16), 16)
 
     def step_of(g, s):
         return s if g == 0 else s + SPLIT
 
     def transit(g, s, way):
-        here, cols = rows(block_z(2) + way * GRP, GRP), pl.ds(*GROUPS[g])
-        return remote(
-            PS.at[s, here, cols], TR.at[way, s, :, cols], sent.at[7], tr_recv.at[step_of(g, s)], to_z(way)
+        cols = pl.ds(*GROUPS[g])
+        return remote(
+            PS.at[s, way, block_z(2), cols], TR.at[way, s, :, cols], sent.at[7], tr_recv.at[step_of(g, s)], to_z(way)
         )
 
     def rs_copy(g, s, way):
-        here, cols = rows(block_z((1, 3)[way]), 64), pl.ds(*GROUPS[g])
-        return remote(
-            PS.at[s, here, cols], RR.at[way, s, :, cols], sent.at[8], rs_recv.at[step_of(g, s)], to_z(way)
+        cols = pl.ds(*GROUPS[g])
+        return remote(
+            PS.at[s, :, block_z((1, 3)[way]), cols], RR.at[way, s, :, :, cols], sent.at[8],
+            rs_recv.at[step_of(g, s)], to_z(way),
         )
 
     def x_copy(g, s):
@@ -219,16 +226,44 @@
         return remote(XS.at[s, :, cols], XR.at[s, :, cols], sent.at[9], x_recv.at[step_of(g, s)], (at_d(0, 1), f))
 
     def s_copy(g, s):
-        mine = SL.at[s, rows(d * GRP, GRP), pl.ds(*GROUPS[g])]
+        mine = SL.at[s, xh, block_z(0), pl.ds(*GROUPS[g])]
         return remote(mine, mine, sent.at[10], s_recv.at[step_of(g, s)], (at_d(0, 1), f))
 
     def z_copy(g, s, way):
-        mine = SL.at[s, rows(z * 64, 64), pl.ds(*GROUPS[g])]
+        mine = SL.at[s, :, block_z(0), pl.ds(*GROUPS[g])]
         return remote(mine, mine, sent.at[11], z_recv.at[step_of(g, s)], to_z(way))
 
     def z_on(g, s, way):
-        here = SL.at[s, rows(block_z((3, 1)[way]) + way * GRP, GRP), pl.ds(*GROUPS[g])]
+        here = SL.at[s, way, block_z((3, 1)[way]), pl.ds(*GROUPS[g])]
         return remote(here, here, sent.at[12], on_recv.at[step_of(g, s)], to_z(way))
+
+    def b_cross(s):
+        return remote(
+            PS.at[s, 1 - xh], XB.at[lax.div(s, B_EVERY)], sent.at[14], tr_recv.at[step_of(3, s)], (at_d(0, 1), f)
+        )
+
+    def b_transit(s, way):
+        return remote(
+            PS.at[s, xh, part_z(2, way)], TR.at[way, s, pl.ds(0, 16)], sent.at[15], rs_recv.at[step_of(3, s)],
+            to_z(way),
+        )
+
+    def b_rs(s, way):
+        return remote(
+            PS.at[s, xh, block_z((1, 3)[way])], RR.at[way, s, 0], sent.at[16], x_recv.at[step_of(3, s)], to_z(way)
+        )
+
+    def b_z(s, way):
+        mine = SL.at[s, xh, block_z(0)]
+        return remote(mine, mine, sent.at[17], s_recv.at[step_of(3, s)], to_z(way))
+
+    def b_on(s, way):
+        here = SL.at[s, xh, part_z((3, 1)[way], way)]
+        return remote(here, here, sent.at[18], z_recv.at[step_of(3, s)], to_z(way))
+
+    def b_back(s):
+        mine = SL.at[s, xh]
+        return remote(mine, mine, sent.at[19], on_recv.at[step_of(3, s)], (at_d(0, 1), f))
 
     def n_copy(s):
         return remote(NS.at[s], NR.at[f], sent.at[13], got.at[5], (d, piece(s)))
@@ -263,41 +298,75 @@
                 w_wait(1)
                 w_out.start()
 
-        part = jnp.dot(T[q], W[:, cols], preferred_element_type=F32) * SCALE
-        PS[s, :, cols] = part.astype(BF)
-        for way in (0, 1):
-            transit(g, s, way).start()
+        part = jnp.dot(T[q].reshape(8 * GRP, TC), W[:, cols], preferred_element_type=F32) * SCALE
+        PS[s, :, :, cols] = part.astype(BF).reshape(2, 4 * GRP, GROUPS[g][1])
+        if g == 3:
+            b_cross(s).start()
+        else:
+            for way in (0, 1):
+                transit(g, s, way).start()
+
+    def b_merge(g, s):
+        drain(XB.at[0], tr_recv.at[step_of(3, s)])
+        PS[s, xh] = (PS[s, xh].astype(F32) + XB[lax.div(s, B_EVERY)].astype(F32)).astype(BF)
+        for way in (0, 1):
+            b_transit(s, way).start()
+
+    def b_reduce(g, s):
+        drain(TR.at[:, s, pl.ds(0, 16)], rs_recv.at[step_of(3, s)])
+        for way in (0, 1):
+            here = part_z((1, 3)[way], way)
+            PS[s, xh, here] = (PS[s, xh, here].astype(F32) + TR[way, s, pl.ds(0, 16)].astype(F32)).astype(BF)
+            b_rs(s, way).start()
+
+    def b_slope(g, s):
+        drain(TR.at[:, s], x_recv.at[step_of(3, s)])
+        preact = PS[s, xh, block_z(0)].astype(F32) + RR[0, s, 0].astype(F32) + RR[1, s, 0].astype(F32)
+        slope_of(g, s, preact)
+        for way in (0, 1):
+            b_z(s, way).start()
+
+    def b_spread(g, s):
+        drain(TR.at[:, s], s_recv.at[step_of(3, s)])
+        for way in (0, 1):
+            b_on(s, way).start()
+
+    def b_hand(g, s):
+        drain(TR.at[:, s, pl.ds(0, 16)], z_recv.at[step_of(3, s)])
+        b_back(s).start()
 
     def merge(g, s):
         cols = pl.ds(*GROUPS[g])
         drain(TR.at[:, s, :, cols], tr_recv.at[step_of(g, s)])
         for way in (0, 1):
-            here = rows(block_z((1, 3)[way]) + way * GRP, GRP)
-            PS[s, here, cols] = (PS[s, here, cols].astype(F32) + TR[way, s, :, cols].astype(F32)).astype(BF)
+            here = block_z((1, 3)[way])
+            PS[s, way, here, cols] = (PS[s, way, here, cols].astype(F32) + TR[way, s, :, cols].astype(F32)).astype(BF)
             rs_copy(g, s, way).start()
 
     def reduce_z(g, s):
         cols = pl.ds(*GROUPS[g])
-        drain(RR.at[:, s, :, cols], rs_recv.at[step_of(g, s)])
+        drain(RR.at[:, s, :, :, cols], rs_recv.at[step_of(g, s)])
 
         def half(h):
-            own = PS[s, rows(z * 64 + h * GRP, GRP), cols].astype(F32)
-            here = rows(h * GRP, GRP)
-            return own + RR[0, s, here, cols].astype(F32) + RR[1, s, here, cols].astype(F32)
+            own = PS[s, h, block_z(0), cols].astype(F32)
+            return own + RR[0, s, h, :, cols].astype(F32) + RR[1, s, h, :, cols].astype(F32)
 
         XS[s, :, cols] = half(1 - xh).astype(BF)
         x_copy(g, s).start()
         XO[s, :, cols] = half(xh)
 
     def slope(g, s):
+        cols = pl.ds(*GROUPS[g])
+        x_copy(g, s).wait_recv()
+        slope_of(g, s, XO[s, :, cols] + XR[s, :, cols].astype(F32))
+        s_copy(g, s).start()
+
+    def slope_of(g, s, preact):
         q, cols = piece(s), pl.ds(*GROUPS[g])
-        x_copy(g, s).wait_recv()
-        preact = XO[s, :, cols] + XR[s, :, cols].astype(F32)
         gate = jax.nn.sigmoid(preact)
         hidden = preact * gate
         cotangent = COT[rows(q * GRP, GRP), cols].astype(F32)
-        SL[s, rows(d * GRP, GRP), cols] = (cotangent * gate * (1.0 + preact * (1.0 - gate))).astype(BF)
-        s_copy(g, s).start()
+        SL[s, xh, block_z(0), cols] = (cotangent * gate * (1.0 + preact * (1.0 - gate))).astype(BF)
         square = hidden * hidden
         total = square[:, :128]
         for j in range(1, GROUPS[g][1] // 128):
@@ -321,37 +390,57 @@
             z_copy(g, s, way).start()
 
     def hand_on(g, s):
-        drain(RR.at[:, s, :, pl.ds(*GROUPS[g])], z_recv.at[step_of(g, s)])
+        drain(RR.at[:, s, :, :, pl.ds(*GROUPS[g])], z_recv.at[step_of(g, s)])
         for way in (0, 1):
             z_on(g, s, way).start()
 
     def gradient(g, s):
         q, cols = piece(s), pl.ds(*GROUPS[g])
-        drain(TR.at[:, s, :, cols], on_recv.at[step_of(g, s)])
+        drain(XB.at[0] if g == 3 else TR.at[:, s, :, cols], on_recv.at[step_of(g, s)])
 
         def tile(m, _):
             here = pl.ds(pl.multiple_of(m * 256, 256), 256)
             ACC[here, cols] += lax.dot_general(
-                T[q, :, here], SL[s, :, cols], (((0,), (0,)), ((), ())), preferred_element_type=F32
+                T[q, :, :, here].reshape(8 * GRP, 256), SL[s, :, :, cols].reshape(8 * GRP, GROUPS[g][1]),
+                (((0,), (0,)), ((), ())), preferred_element_type=F32,
             )
+            if g >= 2:
+
+                @pl.when(s == NF - 1)
+                def _():
+                    pltpu.make_async_copy(ACC.at[here], out_g.at[here], own_sem.at[4]).start()
+
             return 0
 
         lax.fori_loop(0, TC // 256, tile, 0)
 
-    def when_in(i, run):
-        for g, first, last, less in ((0, 0, SPLIT, 0), (1, SPLIT, 2 * SPLIT, SPLIT), (2, 2 * SPLIT, STEPS, SPLIT)):
-
-            @pl.when((i >= first) & (i < last))
-            def _():
-                run(g, i - less)
+    def when_in(i, run, b_run):
+        b_stage = lax.rem(i + STEPS, B_EVERY) == (B_AT + SPLIT + STEPS) % B_EVERY
+        full = (i >= 2 * SPLIT) & (i < STEPS)
+
+        @pl.when((i >= 0) & (i < SPLIT))
+        def _():
+            run(0, i)
+
+        @pl.when((i >= SPLIT) & (i < 2 * SPLIT))
+        def _():
+            run(1, i - SPLIT)
+
+        @pl.when(full & jnp.logical_not(b_stage))
+        def _():
+            run(2, i - SPLIT)
+
+        @pl.when(full & b_stage)
+        def _():
+            b_run(3, i - SPLIT)
 
     def stage(i, _):
-        when_in(i, forward)
-        when_in(i - LAG_M, merge)
-        when_in(i - LAG_X, reduce_z)
-        when_in(i - LAG_S, slope)
-        when_in(i - LAG_Z, spread_z)
-        when_in(i - LAG_H, hand_on)
+        when_in(i, forward, forward)
+        when_in(i - LAG_M, merge, b_merge)
+        when_in(i - LAG_X, reduce_z, b_reduce)
+        when_in(i - LAG_S, slope, b_slope)
+        when_in(i - LAG_Z, spread_z, b_spread)
+        when_in(i - LAG_H, hand_on, b_hand)
         tokens_on(i - SPLIT + TOKEN_LEAD)
 
         @pl.when(i == 0)
@@ -373,17 +462,14 @@
                 near = jnp.where(dy == 1, 0, jnp.where(dy == 3, 1, 2))
                 send_state(u, old, dst, jnp.where(dy == 0, 0, 4 + 4 * dxl + 2 * near) + 2 * dxl + dc)
 
-        when_in(i - LAG_G, gradient)
+        when_in(i - LAG_G, gradient, gradient)
         return 0
 
     lax.fori_loop(0, STEPS + LAG_G, stage, 0)
 
-    g_out = pltpu.make_async_copy(ACC, out_g, own_sem.at[4])
-    g_out.start()
-
     drain(NR.at[pl.ds(0, NF - 1)], got.at[5])
-    square = jnp.sum(jnp.sum(NR[...], axis=0), axis=1, keepdims=True)
-    out_n[...] = jnp.broadcast_to(jnp.sqrt(square / FF + 1e-06), (GRP, 128))
+    square = jnp.sum(jnp.sum(NR[...], axis=0), axis=1)
+    out_n[...] = jnp.sqrt(square / FF + 1e-06)
 
     w_out.wait()
     own_state(1, out_m).wait()
@@ -395,17 +481,24 @@
     drain(CB.at[1, others], sent.at[1])
     drain(CB.at[2, others], sent.at[2])
     drain(CB.at[0, others, :, pl.ds(*GROUPS[1])], sent.at[3])
-    drain(T.at[0, pl.ds(0, 7 * GRP)], sent.at[4])
+    drain(T.at[0, :, pl.ds(0, 7 * GRP // 2)], sent.at[4])
     drain(T.at[pl.ds(0, 9)], sent.at[5])
     drain(T.at[pl.ds(0, 6)], sent.at[6])
-    drain(TR, sent.at[7])
-    drain(RR, sent.at[8])
-    drain(XS, sent.at[9])
-    drain(XS, sent.at[10])
-    drain(RR, sent.at[11])
-    drain(TR, sent.at[12])
+    plain, crossed = pl.ds(0, NF - NB), pl.ds(0, NB)
+    drain(TR.at[:, plain], sent.at[7])
+    drain(RR.at[:, plain], sent.at[8])
+    drain(XS.at[plain], sent.at[9])
+    drain(XS.at[plain], sent.at[10])
+    drain(RR.at[:, plain], sent.at[11])
+    drain(TR.at[:, plain], sent.at[12])
+    drain(XB.at[crossed], sent.at[14])
+    drain(TR.at[:, crossed, pl.ds(0, 16)], sent.at[15])
+    drain(TR.at[:, crossed], sent.at[16])
+    drain(TR.at[:, crossed], sent.at[17])
+    drain(TR.at[:, crossed, pl.ds(0, 16)], sent.at[18])
+    drain(XB.at[crossed], sent.at[19])
     drain(NS.at[others], sent.at[13])
-    g_out.wait()
+    drain(ACC, own_sem.at[4])
 
 
 def update_kernel(w, m, v, g, new_w, new_m, new_v):
@@ -428,27 +521,28 @@
         out_shape=(
             tile, tile, tile,
             jax.ShapeDtypeStruct((TC, FC), F32),
-            jax.ShapeDtypeStruct((GRP, 128), F32),
+            jax.ShapeDtypeStruct((GRP,), F32),
         ),
         in_specs=[anywhere] * 5,
         out_specs=(anywhere, anywhere, anywhere, anywhere, vmem),
         scratch_shapes=[
-            pltpu.VMEM((NF, 8 * GRP, TC), BF),
+            pltpu.VMEM((NF, 2, 4 * GRP, TC), BF),
             pltpu.VMEM((TC, FC), BF),
-            pltpu.VMEM((NF, 8 * GRP, FC), BF),
+            pltpu.VMEM((NF, 2, 4 * GRP, FC), BF),
             pltpu.VMEM((2, NF, GRP, FC), BF),
-            pltpu.VMEM((2, NF, 64, FC), BF),
+            pltpu.VMEM((2, NF, 2, GRP, FC), BF),
             pltpu.VMEM((NF, GRP, FC), F32),
             pltpu.VMEM((NF, GRP, FC), BF),
             pltpu.VMEM((NF, GRP, FC), BF),
-            pltpu.VMEM((NF, 8 * GRP, FC), BF),
+            pltpu.VMEM((-(-NF // B_EVERY), 4 * GRP, FC), BF),
+            pltpu.VMEM((NF, 2, 4 * GRP, FC), BF),
             pltpu.VMEM((TC, FC), F32),
             pltpu.VMEM((2, NF, SR, FC), F32),
             pltpu.VMEM((3, NF, SR, FC), BF),
             pltpu.VMEM((NF, GRP, 128), F32),
             pltpu.VMEM((NF, GRP, 128), F32),
             pltpu.VMEM((8 * SR, FC), BF),
-            dma((3,)), dma((6,)), dma((14,)), dma((6,)), dma((NF,)),
+            dma((3,)), dma((6,)), dma((20,)), dma((6,)), dma((NF,)),
             dma((STEPS,)), dma((STEPS,)), dma((STEPS,)), dma((STEPS,)), dma((STEPS,)), dma((STEPS,)),
         ],
         compiler_params=pltpu.CompilerParams(
@@ -469,7 +563,7 @@
         compiler_params=pltpu.CompilerParams(vmem_limit_bytes=UPD_LIMIT),
         name="adamw_update",
     )(w, m, v, g)
-    return new_weight, new_first, new_second, n[:, 0]
+    return new_weight, new_first, new_second, n
 
 
 def solution(mesh):

time: 182 us -> 178 us (0.978)
  Pallas kernels: 180 us -> 177 us
    pallas_call x1, Pallas kernels: 171 us -> 169 us  [body(): pl.pallas_call(step_kernel, out_shape=(tile, tile, tile, jax.ShapeDtypeSt...]
where the time goes in v4:
time: 178 us
  Pallas kernels  177 us (99%)
    pallas_call x1, Pallas kernels, body(): pl.pallas_call(step_kernel, out_shape=(tile, tile, tile, jax.ShapeDtypeSt...  169 us
    pallas_call x1, Pallas kernels, body(): pl.pallas_call(update_kernel, grid=(TC // rows,), out_shape=(shape, shape...  8.2 us

profile of v4, /device:TPU:0, one launch (start us, length us, event | category | flops | bytes accessed | tf_op | source)
XLA Modules:
  0.0 177.9 jit_solution(11716489988831212863)
XLA Ops:
  0.6 168.6 %train_step.1 = (bf16[1024,896]{1,0:T(8,128)(2,1)}, bf16[1024,896]{1,0:T(8,128)(2,1)}, bf16[1024,896]{1,0:T(8,128)(2,1)}, f32[1024,896]{1,0:T(8,128)}, f32[32]{0:T(128)}) custom-call(bf16[32,8192]{1,0:T(8,128)(2,1)} %tok.1, bf16[512,896]{1,0:T(8,128)(2,1)} %cot.1, f32[64,14336]{1,0:T(8,128)} %old_w.1, f32[64,14336]{1,0:T(8,128)} %old_m.1, f32[64,14336]{1,0:T(8,128)} %old_v.1), custom_call_target="tpu_custom_call" | custom-call | tf_op jit(solution)/shard_map/train_step/pallas_call | solution.py:519
  169.2 0.0 copy-start
  169.2 8.2 %adamw_update.1 = (f32[1024,896]{1,0:T(8,128)}, f32[1024,896]{1,0:T(8,128)}, f32[1024,896]{1,0:T(8,128)}) custom-call(bf16[1024,896]{1,0:T(8,128)(2,1)} %get-tuple-element.12.w, bf16[1024,896]{1,0:T(8,128)(2,1)} %get-tuple-element.13.m, bf16[1024,896]{1,0:T(8,128)(2,1)} %get-tuple-element.14.v, f32[1024,896]{1,0:T(8,128)} %get-tuple-element.15.g), custom_call_target="tpu_custom_call" | custom-call | tf_op jit(solution)/shard_map/adamw_update/pallas_call | solution.py:557
  177.4 0.0 copy-done
  177.4 0.5 copy.10
Async XLA Ops:
  169.2 8.2 %copy-start = (f32[32]{0:T(128)S(1)}, f32[32]{0:T(128)}, u32[]{:S(2)}) copy-start(f32[32]{0:T(128)} %get-tuple-element.27) | copy-start | bytes 388

commit v5 on v4

--- a/solution.py
+++ b/solution.py
@@ -27,17 +27,18 @@
 TOKEN_LEAD = 2
 LAGS = (1, 2, 3, 4, 5, 7)
 LAG_M, LAG_X, LAG_S, LAG_Z, LAG_H, LAG_G = LAGS
-STATES_AT = 5
+STATES_AT = 4
 MESH = pl.DeviceIdType.MESH
 BF, F32 = jnp.bfloat16, jnp.float32
 
 
 def step_kernel(
     tok, cot, old_w, old_m, old_v,
-    out_w, out_m, out_v, out_g, out_n,
+    out_states, out_g, out_n,
     T, W, PS, TR, RR, XO, XS, XR, XB, SL, ACC, ST, CB, NS, NR, COT,
     ld_sem, own_sem, sent, got, tk_recv, tr_recv, rs_recv, x_recv, s_recv, z_recv, on_recv,
 ):
+    out_w, out_m, out_v = (out_states.at[j] for j in range(3))
     d, f = lax.axis_index("dp"), lax.axis_index("fsdp")
     z, xh = lax.div(d, 2), lax.rem(d, 2)
     y, xl, c = lax.div(f, 4), lax.rem(lax.div(f, 2), 2), lax.rem(f, 2)
@@ -501,10 +502,10 @@
     drain(ACC, own_sem.at[4])
 
 
-def update_kernel(w, m, v, g, new_w, new_m, new_v):
-    weight, grad = w[...].astype(F32), g[...] * SCALE
-    first = 0.9 * m[...].astype(F32) + 0.1 * grad
-    second = 0.95 * v[...].astype(F32) + 0.05 * grad * grad
+def update_kernel(states, g, new_w, new_m, new_v):
+    weight, grad = states[0].astype(F32), g[...] * SCALE
+    first = 0.9 * states[1].astype(F32) + 0.1 * grad
+    second = 0.95 * states[2].astype(F32) + 0.05 * grad * grad
     new_m[...] = first
     new_v[...] = second
     update = first * (1.0 / (1.0 - 0.9**10)) / (jnp.sqrt(second * (1.0 / (1.0 - 0.95**10))) + 1e-08)
@@ -514,17 +515,16 @@
 def body(old_weight, old_first, old_second, tokens, cotangent):
     anywhere = pl.BlockSpec(memory_space=pl.ANY)
     vmem = pl.BlockSpec(memory_space=pltpu.VMEM)
-    tile = jax.ShapeDtypeStruct((TC, FC), BF)
     dma = pltpu.SemaphoreType.DMA
-    w, m, v, g, n = pl.pallas_call(
+    states, g, n = pl.pallas_call(
         step_kernel,
         out_shape=(
-            tile, tile, tile,
+            jax.ShapeDtypeStruct((3, TC, FC), BF),
             jax.ShapeDtypeStruct((TC, FC), F32),
             jax.ShapeDtypeStruct((GRP,), F32),
         ),
         in_specs=[anywhere] * 5,
-        out_specs=(anywhere, anywhere, anywhere, anywhere, vmem),
+        out_specs=(anywhere, anywhere, vmem),
         scratch_shapes=[
             pltpu.VMEM((NF, 2, 4 * GRP, TC), BF),
             pltpu.VMEM((TC, FC), BF),
@@ -558,11 +558,11 @@
         update_kernel,
         grid=(TC // rows,),
         out_shape=(shape, shape, shape),
-        in_specs=[block] * 4,
+        in_specs=[pl.BlockSpec((3, rows, FC), lambda i: (0, i, 0)), block],
         out_specs=(block, block, block),
         compiler_params=pltpu.CompilerParams(vmem_limit_bytes=UPD_LIMIT),
         name="adamw_update",
-    )(w, m, v, g)
+    )(states, g)
     return new_weight, new_first, new_second, n
 
 

time: 178 us -> 178 us (level)
  no operation moved by 1% of the time
where the time goes in v5:
time: 178 us; the launch traced here: 177 us
  Pallas kernels  176 us (99%)
    pallas_call x1, Pallas kernels, body(): pl.pallas_call(step_kernel, out_shape=(jax.ShapeDtypeStruct((3, TC, FC),...  168 us
    pallas_call x1, Pallas kernels, body(): pl.pallas_call(update_kernel, grid=(TC // rows,), out_shape=(shape, shape...  8.18 us

profile of v5, /device:TPU:0, one launch (start us, length us, event | category | flops | bytes accessed | tf_op | source)
XLA Modules:
  0.0 177.3 jit_solution(6610117173478103083)
XLA Ops:
  0.6 167.9 %train_step.1 = (bf16[3,1024,896]{2,1,0:T(8,128)(2,1)}, f32[1024,896]{1,0:T(8,128)}, f32[32]{0:T(128)}) custom-call(bf16[32,8192]{1,0:T(8,128)(2,1)} %tok.1, bf16[512,896]{1,0:T(8,128)(2,1)} %cot.1, f32[64,14336]{1,0:T(8,128)} %old_w.1, f32[64,14336]{1,0:T(8,128)} %old_m.1, f32[64,14336]{1,0:T(8,128)} %old_v.1), custom_call_target="tpu_custom_call" | custom-call | tf_op jit(solution)/shard_map/train_step/pallas_call | solution.py:519
  168.5 0.0 copy-start
  168.6 8.2 %adamw_update.1 = (f32[1024,896]{1,0:T(8,128)}, f32[1024,896]{1,0:T(8,128)}, f32[1024,896]{1,0:T(8,128)}) custom-call(bf16[3,1024,896]{2,1,0:T(8,128)(2,1)} %get-tuple-element.10.states, f32[1024,896]{1,0:T(8,128)} %get-tuple-element.11.g), custom_call_target="tpu_custom_call" | custom-call | tf_op jit(solution)/shard_map/adamw_update/pallas_call | solution.py:557
  176.7 0.0 copy-done
  176.7 0.5 copy.10
Async XLA Ops:
  168.5 8.2 %copy-start = (f32[32]{0:T(128)S(1)}, f32[32]{0:T(128)}, u32[]{:S(2)}) copy-start(f32[32]{0:T(128)} %get-tuple-element.23) | copy-start | bytes 388
